TPU v7x, 256 devices: a whole 4x4x8 slice. The times are simulated.
256 devices in a mesh: mp: 16 (over y, x_hi, core), seq: 8 (over z), dp: 2 (over x_lo).
Axes of the slice: x: 4 (x_hi: 2, x_lo: 2; x = x_hi * 2 + x_lo), y: 4, z: 8, core: 2. Of those that a mesh axis runs over, the one named last changes fastest.
Arguments:
- query_rows: bfloat16 [2, 1536, 2048], P('dp', 'seq'), may hold values from -6 to 6
- key_rows: bfloat16 [2, 1536, 2048], P('dp', 'seq'), may hold values from -6 to 6
- value_rows: bfloat16 [2, 1536, 2048], P('dp', 'seq'), may hold values from -6 to 6
- cotangent: bfloat16 [2, 1536, 2048], P('dp', 'seq'), may hold values from -0.15625 to 0.15625
- inner_rate: float32 [2, 1536], P('dp', 'seq'), may hold values from 0.00013950893 to 0.0013950893
- expand_master: float32 [2048, 8192], P(('seq', 'dp'), 'mp'), may hold values from -0.125 to 0.125
- reduce_master: float32 [8192, 2048], P('mp', ('seq', 'dp')), may hold values from -0.0625 to 0.0625
- expand_first: float32 [2048, 8192], P(('seq', 'dp'), 'mp'), may hold values from -1.25 to 1.25
- reduce_first: float32 [8192, 2048], P('mp', ('seq', 'dp')), may hold values from -1.25 to 1.25
- expand_second: float32 [2048, 8192], P(('seq', 'dp'), 'mp'), may hold values from 0.001 to 0.003
- reduce_second: float32 [8192, 2048], P('mp', ('seq', 'dp')), may hold values from 0.001 to 0.003
Outputs:
- mixed: bfloat16 [2, 1536, 2048], P('dp', 'seq', 'mp')
- expand_updated: float32 [2048, 8192], P(('seq', 'dp'), 'mp')
- reduce_updated: float32 [8192, 2048], P('mp', ('seq', 'dp'))
- expand_momentum: float32 [2048, 8192], P(('seq', 'dp'), 'mp')
- reduce_momentum: float32 [8192, 2048], P('mp', ('seq', 'dp'))
- expand_variance: float32 [2048, 8192], P(('seq', 'dp'), 'mp')
- reduce_variance: float32 [8192, 2048], P('mp', ('seq', 'dp'))
- expand_weights: bfloat16 [2048, 8192], P(None, 'mp')
- reduce_weights: bfloat16 [8192, 2048], P('mp')
All inputs are finite; a program needn't handle non-finite values.
Results may differ from a plain program's by a relative error of at most 0.017.
Values may be sent and summed in bfloat16 or wider, within the bound.
A program may use at most 128 MiB of HBM per device.

v0:
```python
import jax
import jax.numpy as jnp
from jax import lax
from jax.sharding import PartitionSpec as P

STEP = 1000


gelu_scale = 0.7978845608028654
gelu_cubic = 0.044715
beta_first = 0.9
beta_second = 0.999
learn_rate = 0.001
weight_decay = 0.1
adam_eps = 1e-08


def gelu_value(value):
    return 0.5 * value * (1.0 + jnp.tanh(gelu_scale * (value + gelu_cubic * value * value * value)))


def gelu_slope(value):
    inner = jnp.tanh(gelu_scale * (value + gelu_cubic * value * value * value))
    return 0.5 * (1.0 + inner) + 0.5 * value * (1.0 - inner * inner) * gelu_scale * (
        1.0 + 3.0 * gelu_cubic * value * value
    )


def adam_update(master, first, second, grad):
    momentum = beta_first * first + (1.0 - beta_first) * grad
    variance = beta_second * second + (1.0 - beta_second) * grad * grad
    first_corr = 1.0 - beta_first**STEP
    second_corr = 1.0 - beta_second**STEP
    updated = master - learn_rate * (
        momentum / first_corr / (jnp.sqrt(variance / second_corr) + adam_eps)
        + weight_decay * master
    )
    return (updated, momentum, variance)


def body(
    query_rows,
    key_rows,
    value_rows,
    cotangent,
    inner_rate,
    expand_master,
    reduce_master,
    expand_first,
    reduce_first,
    expand_second,
    reduce_second,
):
    expand_fast, reduce_fast = (
        lax.all_gather(expand_master.astype(jnp.bfloat16), ("seq", "dp"), axis=0, tiled=True),
        lax.all_gather(reduce_master.astype(jnp.bfloat16), ("seq", "dp"), axis=1, tiled=True),
    )
    queries = query_rows[0]
    keys = key_rows[0]
    values = value_rows[0]
    upstream = cotangent[0]
    rates = inner_rate[0]
    length = keys.shape[0]
    hidden = jnp.dot(keys, expand_fast, preferred_element_type=jnp.float32)
    act = gelu_value(hidden)
    act_b = act.astype(jnp.bfloat16)
    partial_recon = jnp.dot(act_b, reduce_fast, preferred_element_type=jnp.float32)
    recon = lax.psum(partial_recon, "mp")
    resid = keys.astype(jnp.float32) + recon - values.astype(jnp.float32)
    resid_b = resid.astype(jnp.bfloat16)
    d_hidden = jnp.dot(resid_b, reduce_fast.T, preferred_element_type=jnp.float32) * gelu_slope(
        hidden
    )
    dz_w = (rates[:, None] * d_hidden).astype(jnp.bfloat16)
    act_w = (rates[:, None] * act).astype(jnp.bfloat16)
    all_keys, all_dz, all_act, all_resid = (
        lax.all_gather(keys, "seq", axis=0, tiled=True),
        lax.all_gather(dz_w, "seq", axis=0, tiled=True),
        lax.all_gather(act_w, "seq", axis=0, tiled=True),
        lax.all_gather(resid_b, "seq", axis=0, tiled=True),
    )
    places = lax.axis_index("seq") * length + jnp.arange(length, dtype=jnp.int32)
    earlier = jnp.arange(all_keys.shape[0], dtype=jnp.int32)
    causal = places[:, None] >= earlier[None, :]
    first_score = jnp.where(
        causal, jnp.dot(queries, all_keys.T, preferred_element_type=jnp.float32), 0.0
    ).astype(jnp.bfloat16)
    zq = jnp.dot(queries, expand_fast, preferred_element_type=jnp.float32) - jnp.dot(
        first_score, all_dz, preferred_element_type=jnp.float32
    )
    aq_b = gelu_value(zq).astype(jnp.bfloat16)
    second_score = jnp.where(
        causal, jnp.dot(aq_b, all_act.T, preferred_element_type=jnp.float32), 0.0
    ).astype(jnp.bfloat16)
    partial_mixed = jnp.dot(aq_b, reduce_fast, preferred_element_type=jnp.float32) - jnp.dot(
        second_score, all_resid, preferred_element_type=jnp.float32
    )
    mixed_share = lax.psum_scatter(partial_mixed, "mp", scatter_dimension=1, tiled=True)
    feature_count = mixed_share.shape[1]
    own_queries = lax.dynamic_slice_in_dim(
        queries, lax.axis_index("mp") * feature_count, feature_count, 1
    )
    mixed = (own_queries.astype(jnp.float32) + mixed_share).astype(jnp.bfloat16)[None]
    reduce_grad = jnp.dot(aq_b.T, upstream, preferred_element_type=jnp.float32)
    third_score = jnp.where(
        causal, jnp.dot(upstream, all_resid.T, preferred_element_type=jnp.float32), 0.0
    ).astype(jnp.bfloat16)
    d_act = jnp.dot(upstream, reduce_fast.T, preferred_element_type=jnp.float32) - jnp.dot(
        third_score, all_act, preferred_element_type=jnp.float32
    )
    dzq_b = (d_act * gelu_slope(zq)).astype(jnp.bfloat16)
    expand_grad = jnp.dot(queries.T, dzq_b, preferred_element_type=jnp.float32)
    expand_owned, reduce_owned = (
        lax.psum_scatter(expand_grad, ("seq", "dp"), scatter_dimension=0, tiled=True),
        lax.psum_scatter(reduce_grad, ("seq", "dp"), scatter_dimension=1, tiled=True),
    )
    expand_updated, expand_momentum, expand_variance = adam_update(
        expand_master, expand_first, expand_second, expand_owned
    )
    reduce_updated, reduce_momentum, reduce_variance = adam_update(
        reduce_master, reduce_first, reduce_second, reduce_owned
    )
    expand_weights, reduce_weights = (
        lax.all_gather(expand_updated.astype(jnp.bfloat16), ("seq", "dp"), axis=0, tiled=True),
        lax.all_gather(reduce_updated.astype(jnp.bfloat16), ("seq", "dp"), axis=1, tiled=True),
    )
    return (
        mixed,
        expand_updated,
        reduce_updated,
        expand_momentum,
        reduce_momentum,
        expand_variance,
        reduce_variance,
        expand_weights,
        reduce_weights,
    )


def solution(mesh):
    in_specs = (
        P("dp", "seq", None),
        P("dp", "seq", None),
        P("dp", "seq", None),
        P("dp", "seq", None),
        P("dp", "seq"),
        P(("seq", "dp"), "mp"),
        P("mp", ("seq", "dp")),
        P(("seq", "dp"), "mp"),
        P("mp", ("seq", "dp")),
        P(("seq", "dp"), "mp"),
        P("mp", ("seq", "dp")),
    )
    out_specs = (
        P("dp", "seq", "mp"),
        P(("seq", "dp"), "mp"),
        P("mp", ("seq", "dp")),
        P(("seq", "dp"), "mp"),
        P("mp", ("seq", "dp")),
        P(("seq", "dp"), "mp"),
        P("mp", ("seq", "dp")),
        P(None, "mp"),
        P("mp", None),
    )
    return jax.shard_map(body, mesh=mesh, in_specs=in_specs, out_specs=out_specs, check_vma=False)
```

profile of v0, /device:TPU:2, one launch (start us, length us, event | category | flops | bytes accessed | tf_op | source)
XLA Modules:
  0.0 1028.7 jit_solution(15143861702710844366)
XLA Ops:
  7.2 1.7 convert_element_type.59
  8.9 0.0 all-gather.12.cloned.1.call-start
  9.0 1.6 convert_element_type.63
  10.6 0.0 all-reduce.2.cloned.1.call-start
  10.7 74.3 %all-gather.10.cloned.1.call-done = bf16[2048,512]{1,0:T(8,128)(2,1)} async-done(((bf16[128,512]{1,0:T(8,128)(2,1)}), bf16[2048,512]{1,0:T(8,128)(2,1)}) %all-gather.10.cloned.1.call-update) | async-done | bytes 2097168 | tf_op jit(solution)/shard_map/all_gather | solution.py:55
  85.0 3.1 multiply_convert_fusion
  88.2 82.0 %all-gather.12.cloned.1.call-done = bf16[512,2048]{1,0:T(8,128)(2,1)} async-done(((bf16[512,128]{1,0:T(8,128)(2,1)}), bf16[512,2048]{1,0:T(8,128)(2,1)}) %all-gather.12.cloned.1.call-update) | async-done | bytes 2097168 | tf_op jit(solution)/shard_map/all_gather | solution.py:56
  170.2 3.4 fusion.57
  173.6 0.0 all-gather.14.cloned.1.call-start
  173.7 147.7 %all-reduce.2.cloned.1.call-done = f32[192,2048]{1,0:T(8,128)} async-done(((f32[192,2048]{1,0:T(8,128)}), f32[192,2048]{1,0:T(8,128)}) %all-reduce.2.cloned.1.call-update) | async-done | bytes 1572880 | tf_op jit(solution)/shard_map/psum | solution.py:68
  321.3 3.0 fusion.11
  324.4 2.8 fusion.14
  327.2 0.0 all-gather.24.cloned.1.call-start
  327.3 0.5 all-gather.24.cloned.1.call-update
  327.9 0.5 all-gather.18.cloned.1.call-update
  328.4 0.7 all-gather.16.cloned.1.call-update
  329.2 3.2 fusion.29
  332.4 36.5 %all-gather.14.cloned.1.call-done = bf16[1536,512]{1,0:T(8,128)(2,1)} async-done(((bf16[192,512]{1,0:T(8,128)(2,1)}), bf16[1536,512]{1,0:T(8,128)(2,1)}) %all-gather.14.cloned.1.call-update) | async-done | bytes 1572880 | tf_op jit(solution)/shard_map/all_gather | solution.py:78
  368.9 74.9 %all-gather.24.cloned.1.call-done = bf16[1,1536,2048]{2,1,0:T(8,128)(2,1)} async-done(((bf16[1,192,2048]{2,1,0:T(8,128)(2,1)}), bf16[1,1536,2048]{2,1,0:T(8,128)(2,1)}) %all-gather.24.cloned.1.call-update) | async-done | bytes 6291472 | tf_op jit(solution)/shard_map/all_gather | solution.py:77
  443.8 6.1 convolution_subtract_fusion.2
  449.9 2.8 fusion.19
  452.7 0.0 reduce-scatter.6.cloned.1.call-start
  452.8 1.6 fusion.22
  454.4 64.9 %all-gather.18.cloned.1.call-done = bf16[1536,2048]{1,0:T(8,128)(2,1)} async-done(((bf16[192,2048]{1,0:T(8,128)(2,1)}), bf16[1536,2048]{1,0:T(8,128)(2,1)}) %all-gather.18.cloned.1.call-update) | async-done | bytes 6291472 | tf_op jit(solution)/shard_map/all_gather | solution.py:80
  519.3 5.8 fusion.9
  525.1 35.3 %all-gather.16.cloned.1.call-done = bf16[1536,512]{1,0:T(8,128)(2,1)} async-done(((bf16[192,512]{1,0:T(8,128)(2,1)}), bf16[1536,512]{1,0:T(8,128)(2,1)}) %all-gather.16.cloned.1.call-update) | async-done | bytes 1572880 | tf_op jit(solution)/shard_map/all_gather | solution.py:79
  560.4 5.3 convolution_bitcast_fusion
  565.7 0.0 reduce-scatter.4.cloned.1.call-start
  565.7 6.3 fusion.16
  572.1 3.3 convolution_subtract_fusion
  575.5 0.0 all-gather.22.cloned.1.call-start
  575.5 84.6 %reduce-scatter.8.cloned.1.call-done = f32[512,128]{1,0:T(8,128)} async-done(((f32[512,2048]{1,0:T(8,128)}), f32[512,128]{1,0:T(8,128)}) %reduce-scatter.8.cloned.1.call-update) | async-done | bytes 262160 | tf_op jit(solution)/shard_map/reduce_scatter | solution.py:115
  660.2 2.0 fusion.76
  662.2 0.0 all-gather.20.cloned.1.call-start
  662.2 0.1 copy.23
  662.4 0.1 copy.20
  662.5 0.1 copy.21
  662.6 100.4 %reduce-scatter.6.cloned.1.call-done = f32[128,512]{0,1:T(8,128)} async-done(((f32[2048,512]{0,1:T(8,128)}), f32[128,512]{0,1:T(8,128)}) %reduce-scatter.6.cloned.1.call-update) | async-done | bytes 262160 | tf_op jit(solution)/shard_map/reduce_scatter | solution.py:114
  763.0 1.8 fusion.78
  764.9 80.4 %reduce-scatter.4.cloned.1.call-done = f32[192,128]{1,0:T(8,128)} async-done(((f32[192,2048]{1,0:T(8,128)}), f32[192,128]{1,0:T(8,128)}) %reduce-scatter.4.cloned.1.call-update) | async-done | bytes 98320 | tf_op jit(solution)/shard_map/reduce_scatter | solution.py:98
  845.3 1.5 fusion.64
  846.8 84.0 %all-gather.22.cloned.1.call-done = bf16[512,2048]{1,0:T(8,128)(2,1)} async-done(((bf16[512,128]{1,0:T(8,128)(2,1)}), bf16[512,2048]{1,0:T(8,128)(2,1)}) %all-gather.22.cloned.1.call-update) | async-done | bytes 2097168 | tf_op jit(solution)/shard_map/all_gather | solution.py:125
  930.8 0.8 copy.24
  931.7 0.8 copy.25
  932.5 0.8 copy.26
  933.3 83.3 %all-gather.20.cloned.1.call-done = bf16[2048,512]{0,1:T(8,128)(2,1)} async-done(((bf16[128,512]{0,1:T(8,128)(2,1)}), bf16[2048,512]{0,1:T(8,128)(2,1)}) %all-gather.20.cloned.1.call-update) | async-done | bytes 2097168 | tf_op jit(solution)/shard_map/all_gather | solution.py:124
  1016.6 3.9 copy.27
  1020.5 1.3 copy.30
  (34 shorter events, 0.4 us)
Async XLA Ops:
  7.2 442.7 %copy-start = (bf16[1,192,2048]{2,1,0:T(8,128)(2,1)S(1)}, bf16[1,192,2048]{2,1,0:T(8,128)(2,1)}, u32[]{:S(2)}) copy-start(bf16[1,192,2048]{2,1,0:T(8,128)(2,1)} %param.14) | copy-start | bytes 2359300
  7.2 77.8 %all-gather.10.cloned.1.call-start = ((), (), s32[]{:S(2)}) async-start(), calls=%async_computation.3 | async-start | bytes 2228224 | tf_op jit(solution)/shard_map/all_gather | solution.py:55
  8.9 161.2 %all-gather.12.cloned.1.call-start = ((), (), s32[]{:S(2)}) async-start(), calls=%async_computation.4 | async-start | bytes 2228224 | tf_op jit(solution)/shard_map/all_gather | solution.py:56
  10.6 310.7 %all-reduce.2.cloned.1.call-start = ((), (), s32[]{:S(2)}) async-start(), calls=%async_computation.5 | async-start | bytes 3145728 | tf_op jit(solution)/shard_map/psum | solution.py:68
  173.6 150.8 %copy-start.1 = (bf16[512,2048]{1,0:T(8,128)(2,1)S(1)}, bf16[512,2048]{1,0:T(8,128)(2,1)}, u32[]{:S(2)}) copy-start(bf16[512,2048]{1,0:T(8,128)(2,1)} %all-gather.12.cloned.1.call-done) | copy-start | bytes 6291460
  173.6 150.8 %copy-start.9 = (f32[1,192]{1,0:T(1,128)S(1)}, f32[1,192]{1,0:T(1,128)}, u32[]{:S(2)}) copy-start(f32[1,192]{1,0:T(1,128)} %param.15) | copy-start | bytes 2308
  173.6 195.3 %all-gather.14.cloned.1.call-start = ((), (), s32[]{:S(2)}) async-start(), calls=%async_computation.6 | async-start | bytes 1769472 | tf_op jit(solution)/shard_map/all_gather | solution.py:78
  327.2 116.6 %all-gather.24.cloned.1.call-start = ((), (), s32[]{:S(2)}) async-start(), calls=%async_computation.14 | async-start | bytes 7077888 | tf_op jit(solution)/shard_map/all_gather | solution.py:77
  327.8 191.5 %all-gather.18.cloned.1.call-start = ((), (), s32[]{:S(2)}) async-start(), calls=%async_computation.8 | async-start | bytes 7077888 | tf_op jit(solution)/shard_map/all_gather | solution.py:80
  328.4 232.0 %all-gather.16.cloned.1.call-start = ((), (), s32[]{:S(2)}) async-start(), calls=%async_computation.7 | async-start | bytes 1769472 | tf_op jit(solution)/shard_map/all_gather | solution.py:79
  329.1 331.0 %reduce-scatter.8.cloned.1.call-start = ((), (), s32[]{:S(2)}) async-start(), calls=%async_computation.11 | async-start | bytes 4456448 | tf_op jit(solution)/shard_map/reduce_scatter | solution.py:115
  452.7 310.3 %reduce-scatter.6.cloned.1.call-start = ((), (), s32[]{:S(2)}) async-start(), calls=%async_computation.10 | async-start | bytes 4456448 | tf_op jit(solution)/shard_map/reduce_scatter | solution.py:114
  565.7 279.6 %reduce-scatter.4.cloned.1.call-start = ((), (), s32[]{:S(2)}) async-start(), calls=%async_computation.9 | async-start | bytes 1671168 | tf_op jit(solution)/shard_map/reduce_scatter | solution.py:98
  575.4 84.7 %copy-start.3 = (f32[512,128]{1,0:T(8,128)S(1)}, f32[512,128]{1,0:T(8,128)}, u32[]{:S(2)}) copy-start(f32[512,128]{1,0:T(8,128)} %param.17) | copy-start | bytes 786436
  575.4 84.7 %copy-start.5 = (f32[512,128]{1,0:T(8,128)S(1)}, f32[512,128]{1,0:T(8,128)}, u32[]{:S(2)}) copy-start(f32[512,128]{1,0:T(8,128)} %param.21) | copy-start | bytes 786436
  575.4 84.7 %copy-start.6 = (f32[512,128]{1,0:T(8,128)S(1)}, f32[512,128]{1,0:T(8,128)}, u32[]{:S(2)}) copy-start(f32[512,128]{1,0:T(8,128)} %param.19) | copy-start | bytes 786436
  575.4 86.8 %copy-start.4 = (f32[128,512]{1,0:T(8,128)S(1)}, f32[128,512]{1,0:T(8,128)}, u32[]{:S(2)}) copy-start(f32[128,512]{1,0:T(8,128)} %param.16) | copy-start | bytes 786436
  575.4 86.9 %copy-start.7 = (f32[128,512]{1,0:T(8,128)S(1)}, f32[128,512]{1,0:T(8,128)}, u32[]{:S(2)}) copy-start(f32[128,512]{1,0:T(8,128)} %param.18) | copy-start | bytes 786436
  575.5 87.0 %copy-start.8 = (f32[128,512]{1,0:T(8,128)S(1)}, f32[128,512]{1,0:T(8,128)}, u32[]{:S(2)}) copy-start(f32[128,512]{1,0:T(8,128)} %param.20) | copy-start | bytes 786436
  575.5 355.4 %all-gather.22.cloned.1.call-start = ((), (), s32[]{:S(2)}) async-start(), calls=%async_computation.13 | async-start | bytes 2228224 | tf_op jit(solution)/shard_map/all_gather | solution.py:125
  662.2 354.5 %all-gather.20.cloned.1.call-start = ((), (), s32[]{:S(2)}) async-start(), calls=%async_computation.12 | async-start | bytes 2228224 | tf_op jit(solution)/shard_map/all_gather | solution.py:124
  933.3 87.2 %copy-start.2 = (bf16[512,2048]{1,0:T(8,128)(2,1)S(1)}, bf16[512,2048]{1,0:T(8,128)(2,1)}, u32[]{:S(2)}) copy-start(bf16[512,2048]{1,0:T(8,128)(2,1)} %all-gather.22.cloned.1.call-done) | copy-start | bytes 6291460
Sparse Core Ops, SparseCore 0:
  10.4 74.6 all-gather.9
  87.3 82.8 all-gather.11
  173.7 147.5 all-reduce.1
  327.3 41.5 all-gather.13
  370.7 73.0 all-gather.23
  446.2 73.0 all-gather.17
  521.8 38.5 all-gather.15
  563.1 97.0 reduce-scatter.7
  662.9 100.1 reduce-scatter.5
  768.2 77.0 reduce-scatter.3
  847.6 83.2 all-gather.21
  933.0 83.6 all-gather.19
where the time goes:
time: 1030 us
  waiting for transfers between devices  950 us (92%)
  matrix products  43.7 us (4%)
  between operations  14.4 us (1%)
  other arithmetic  11.7 us (1%)
    psum x1, waiting for transfers between devices, body(): recon = lax.psum(partial_recon, 'mp')  148 us
    reduce_scatter x1, waiting for transfers between devices, body(): lax.psum_scatter(expand_grad, ('seq', 'dp'), scatter_dimension=0, tiled=T...  100 us
    reduce_scatter x1, waiting for transfers between devices, body(): lax.psum_scatter(reduce_grad, ('seq', 'dp'), scatter_dimension=1, tiled=T...  84.6 us
    all_gather x1, waiting for transfers between devices, body(): lax.all_gather(reduce_updated.astype(jnp.bfloat16), ('seq', 'dp'), axis=1...  84 us
    all_gather x1, waiting for transfers between devices, body(): lax.all_gather(expand_updated.astype(jnp.bfloat16), ('seq', 'dp'), axis=0...  83.3 us
    all_gather x1, waiting for transfers between devices, body(): lax.all_gather(reduce_master.astype(jnp.bfloat16), ('seq', 'dp'), axis=1,...  82 us
    reduce_scatter x1, waiting for transfers between devices, body(): lax.psum_scatter(partial_mixed, 'mp', scatter_dimension=1, tiled=True)  80.4 us
    all_gather x1, waiting for transfers between devices, body(): lax.all_gather(keys, 'seq', axis=0, tiled=True)  74.9 us
  transfers between devices with their start and end apart: 12, of which 12 were waited for; matrix products, arithmetic and copies ran while one was open for 5% of the time, Pallas kernels for 0%

commit v1 on v0

v1 whole, which is shorter than its diff:
```python
import jax
import jax.numpy as jnp
from jax import lax
from jax.experimental import pallas as pl
from jax.experimental.pallas import tpu as pltpu
from jax.sharding import PartitionSpec as P

STEP = 1000
MESH = pl.DeviceIdType.MESH
F32 = jnp.float32
BF = jnp.bfloat16

gelu_scale = 0.7978845608028654
gelu_cubic = 0.044715
beta_first = 0.9
beta_second = 0.999
learn_rate = 0.001
weight_decay = 0.1
adam_eps = 1e-08

SEQ, DP, MP = 8, 2, 16
ROWS, D, HID = 192, 2048, 512
N_SEMS = 208


def gelu_both(value):
    inner = jnp.tanh(gelu_scale * (value + gelu_cubic * value * value * value))
    act = 0.5 * value * (1.0 + inner)
    slope = 0.5 * (1.0 + inner) + 0.5 * value * (1.0 - inner * inner) * gelu_scale * (
        1.0 + 3.0 * gelu_cubic * value * value
    )
    return act, slope


def adam_update(master, first, second, grad):
    momentum = beta_first * first + (1.0 - beta_first) * grad
    variance = beta_second * second + (1.0 - beta_second) * grad * grad
    first_corr = 1.0 - beta_first**STEP
    second_corr = 1.0 - beta_second**STEP
    updated = master - learn_rate * (
        momentum / first_corr / (jnp.sqrt(variance / second_corr) + adam_eps)
        + weight_decay * master
    )
    return (updated, momentum, variance)


def dot(a, b):
    return jnp.dot(a, b, preferred_element_type=F32)


def dot_nt(a, b):
    return lax.dot_general(a, b, (((1,), (1,)), ((), ())), preferred_element_type=F32)


def dot_tn(a, b):
    return lax.dot_general(a, b, (((0,), (0,)), ((), ())), preferred_element_type=F32)


def mod(a, n):
    return lax.rem(a + 2 * n, n)


class Wire:
    def __init__(self, send, recv):
        self.send, self.recv, self.count, self.sent = send, recv, 0, []

    def slot(self):
        self.count += 1
        assert self.count <= N_SEMS
        return self.count - 1

    def copy(self, src, dst, slot, to):
        return pltpu.make_async_remote_copy(
            src_ref=src,
            dst_ref=dst,
            send_sem=self.send.at[slot],
            recv_sem=self.recv.at[slot],
            device_id=to,
            device_id_type=MESH,
        )

    def start(self, src, dst, slot, to, cond=None):
        def go():
            self.copy(src, dst, slot, to).start()

        guarded(cond, go)
        self.sent.append((src, dst, slot, to, cond))

    def arrive(self, dst, slot, to, cond=None):
        def go():
            self.copy(dst, dst, slot, to).wait_recv()

        guarded(cond, go)

    def drain(self):
        for src, dst, slot, to, cond in self.sent:
            guarded(cond, lambda: self.copy(src, dst, slot, to).wait_send())
        self.sent = []


def guarded(cond, go):
    if cond is None:
        go()
    else:
        pl.when(cond)(go)


class Place:
    def __init__(self):
        self.m = lax.axis_index("mp")
        self.z = lax.axis_index("seq")
        self.d = lax.axis_index("dp")
        self.core = lax.rem(self.m, 2)
        self.chip = self.m // 2
        self.sibling = {"mp": self.chip * 2 + 1 - self.core}
        self.partner = {"dp": 1 - self.d}
        self.up = {"seq": mod(self.z + 1, SEQ)}
        self.down = {"seq": mod(self.z - 1, SEQ)}
        self.low = self.chip < 6

    def peer(self, off):
        return lax.rem(self.chip + off, 8)

    def source(self, off):
        return lax.rem(self.chip + 8 - off, 8)

    def chip_id(self, chip):
        return {"mp": chip * 2 + self.core}


class Ring:
    def __init__(self, w, p, view, cond=None, on_block=None, landing=None):
        self.w, self.p, self.view, self.cond, self.on_block = w, p, view, cond, on_block
        self.ups = [w.slot() for _ in range(4)]
        self.downs = [w.slot() for _ in range(3)]

    def go(self, block, up=None, down=None, src=None):
        ref = self.view(block)
        src = ref if src is None else src
        if up is not None:
            self.w.start(src, ref, self.ups[up], self.p.up, self.cond)
        if down is not None:
            self.w.start(src, ref, self.downs[down], self.p.down, self.cond)

    def start(self, src=None):
        self.go(self.p.z, 0, 0, src)

    def step(self, s):
        b = mod(self.p.z - s, SEQ)
        self.w.arrive(self.view(b), self.ups[s - 1], self.p.up, self.cond)
        if s < 4:
            self.go(b, up=s)
        if self.on_block:
            self.on_block(b, 2 * s - 1)
        if s < 4:
            b = mod(self.p.z + s, SEQ)
            self.w.arrive(self.view(b), self.downs[s - 1], self.p.down, self.cond)
            if s < 3:
                self.go(b, down=s)
            if self.on_block:
                self.on_block(b, 2 * s)


class Spread:
    def __init__(self, w, p, view, low):
        self.w, self.p, self.view, self.low = w, p, view, low
        self.far = [w.slot() for _ in range(8)]
        self.near = [w.slot() for _ in range(8)]

    def cond(self, chip):
        return chip < 6 if self.low else None

    def start(self):
        w, p = self.w, self.p
        own = self.view(p.m)
        for off in range(1, 8):
            w.start(own, own, self.far[off], p.chip_id(p.peer(off)), self.cond(p.chip))
        w.start(own, own, self.near[0], p.sibling, self.cond(p.chip))

    def relay(self):
        w, p = self.w, self.p
        for off in range(1, 8):
            src = p.source(off)
            ref = self.view(src * 2 + p.core)
            w.arrive(ref, self.far[off], p.chip_id(p.peer(off)), self.cond(src))
            w.start(ref, ref, self.near[off], p.sibling, self.cond(src))

    def finish(self):
        w, p = self.w, self.p
        for off in range(8):
            src = p.source(off)
            ref = self.view(src * 2 + 1 - p.core)
            w.arrive(ref, self.near[off], p.sibling, self.cond(src))


class Gather:
    def __init__(self, w, p, parts, near, far, low):
        self.w, self.p, self.parts, self.near, self.far, self.low = w, p, parts, near, far, low
        self.s_near = [w.slot() for _ in range(8)]
        self.s_far = [w.slot() for _ in range(8)]

    def cond(self, chip):
        return chip < 6 if self.low else None

    def compute(self, tile):
        w, p = self.w, self.p
        for off in (1, 2, 3, 4, 5, 6, 7, 0):
            chip = p.peer(off)

            def go():
                both = tile(chip)
                self.parts[0, chip] = both[:, :128].astype(BF)
                self.parts[1, chip] = both[:, 128:].astype(BF)

            guarded(self.cond(chip), go)
            w.start(
                self.parts.at[1 - p.core, chip],
                self.near.at[chip],
                self.s_near[off],
                p.sibling,
                self.cond(chip),
            )

    def relay(self):
        w, p = self.w, self.p
        for off in (1, 2, 3, 4, 5, 6, 7, 0):
            chip = p.peer(off)
            ref = self.near.at[chip]
            w.arrive(ref, self.s_near[off], p.sibling, self.cond(chip))

            def go():
                total = ref[...].astype(F32) + self.parts[p.core, chip].astype(F32)
                self.near[chip] = total.astype(BF)

            guarded(self.cond(chip), go)
            if off:
                w.start(ref, self.far.at[off], self.s_far[off], p.chip_id(chip), self.cond(chip))

    def finish(self):
        w, p = self.w, self.p
        total = self.near[p.chip].astype(F32)
        for off in range(1, 8):
            w.arrive(self.far.at[off], self.s_far[off], p.chip_id(p.peer(off)))
            total = total + self.far[off].astype(F32)
        return total


class Fold:
    def __init__(self, w, p, own, ups, downs):
        self.w, self.p, self.own, self.ups, self.downs = w, p, own, ups, downs
        self.s_up = [w.slot() for _ in range(4)]
        self.s_down = [w.slot() for _ in range(3)]

    def start(self, src_up, src_down):
        self.w.start(src_up, self.ups.at[0], self.s_up[0], self.p.up)
        self.w.start(src_down, self.downs.at[0], self.s_down[0], self.p.down)

    def step(self, s):
        w, p = self.w, self.p
        if s < 4:
            ref = self.ups.at[s - 1]
            w.arrive(ref, self.s_up[s - 1], p.up)
            ref[...] = (ref[...].astype(F32) + self.own(mod(p.z + 4 - s, SEQ))).astype(BF)
            w.start(ref, self.ups.at[s], self.s_up[s], p.up)
        if s < 3:
            ref = self.downs.at[s - 1]
            w.arrive(ref, self.s_down[s - 1], p.down)
            ref[...] = (ref[...].astype(F32) + self.own(mod(p.z - 3 + s, SEQ))).astype(BF)
            w.start(ref, self.downs.at[s], self.s_down[s], p.down)

    def finish(self):
        w, p = self.w, self.p
        w.arrive(self.downs.at[2], self.s_down[2], p.down)
        w.arrive(self.ups.at[3], self.s_up[3], p.up)
        return self.own(p.z) + self.ups[3].astype(F32) + self.downs[2].astype(F32)


def kernel(
    q_ref, k_ref, v_ref, c_ref, rate_ref,
    em_ref, rm_ref, e1_ref, r1_ref, e2_ref, r2_ref,
    mixed_ref, eu_ref, ru_ref, em1_ref, rm1_ref, ev_ref, rv_ref, ew_ref, rw_ref,
    ef, rf, k_rows, r_rows, act_all, dz_all, score1, score3, act_b, slope, resid, qe, cr,
    parts, near, far, parts2, near2, far2, parts3, near3, far3, own2, aq, dzq,
    g_r, x_r, up_r, down_r, g_e, x_e, up_e, down_e, w_e, w_r, send, recv, local,
):
    w, p = Wire(send, recv), Place()
    m, z, d = p.m, p.z, p.d

    barrier = pltpu.get_barrier_semaphore()
    friends = [p.up, p.down, p.partner, p.sibling]
    friends += [p.chip_id(p.peer(off)) for off in range(1, 8)]
    for friend in friends:
        pl.semaphore_signal(barrier, inc=1, device_id=friend, device_id_type=MESH)
    pl.semaphore_wait(barrier, len(friends))

    def e_block(j, dd):
        return pl.ds(pl.multiple_of(j * 256 + dd * 128, 128), 128)

    def e_pair(j):
        return pl.ds(pl.multiple_of(j * 256, 256), 256)

    def weights(full_e, full_r, own_e, own_r, extra):
        s_own, s_r = w.slot(), [w.slot() for _ in range(8)]
        mine = full_e.at[e_block(z, d), :]
        w.start(own_e, mine, s_own, p.partner)

        def forward(block, index, src=None):
            ref = full_r.at[:, e_block(block, d)]
            w.start(ref if src is None else src, ref, s_r[index], p.partner)

        ring_r = Ring(w, p, lambda j: full_r.at[:, e_block(j, d)], on_block=forward)
        ring_e = Ring(w, p, lambda j: full_e.at[e_pair(j), :])
        ring_r.start(own_r)
        forward(z, 0, own_r)
        w.arrive(full_e.at[e_block(z, 1 - d), :], s_own, p.partner)
        ring_e.start()
        for s in range(1, 5):
            extra(s)
            ring_e.step(s)
            ring_r.step(s)

        def finish():
            for index in range(8):
                hop = (index + 1) // 2
                block = mod(z - hop if index % 2 else z + hop, SEQ)
                w.arrive(full_r.at[:, e_block(block, 1 - d)], s_r[index], p.partner)

        return finish

    ef[e_block(z, d), :] = em_ref[...].astype(BF)
    rf[:, e_block(z, d)] = rm_ref[...].astype(BF)
    own_rows = pl.ds(pl.multiple_of(m * 16, 16), 16)

    def take_rows(out, rows_ref):
        def go():
            out[z] = rows_ref[own_rows, :]

        guarded(p.low, go)

    take_rows(k_rows, k_ref)
    ring_k = Ring(w, p, lambda j: k_rows.at[j], cond=p.low)
    ring_k.start()

    t_at = z * ROWS + lax.broadcasted_iota(jnp.int32, (ROWS, 128), 0)
    col = lax.broadcasted_iota(jnp.int32, (ROWS, 128), 1)
    s_at = (col // 16) * ROWS + m * 16 + lax.rem(col, 16)
    causal = t_at >= s_at

    def block_of(ref, block):
        return ref.at[:, pl.ds(pl.multiple_of(block * 128, 128), 128)]

    spread1 = Spread(w, p, lambda b: block_of(score1, b), True)
    spread_r = Spread(w, p, lambda b: block_of(resid, b), False)
    spread3 = Spread(w, p, lambda b: block_of(score3, b), True)

    def score(rows_ref, others, out):
        def go():
            part = dot_nt(rows_ref[...], others[...].reshape(128, D))
            block_of(out, m)[...] = jnp.where(causal, part, 0.0).astype(BF)

        guarded(p.low, go)

    def extra(s):
        ring_k.step(s)
        if s == 4:
            score(q_ref, k_rows, score1)
            spread1.start()

    mine_e, mine_r = ef.at[e_block(z, d), :], rf.at[:, e_block(z, d)]
    finish_weights = weights(ef, rf, mine_e, mine_r, extra)

    eye = lax.broadcasted_iota(jnp.int32, (ROWS, ROWS), 0) == lax.broadcasted_iota(
        jnp.int32, (ROWS, ROWS), 1
    )
    rates = jnp.sum(jnp.where(eye, rate_ref[...], 0.0), axis=1, keepdims=True)

    def put(ref, columns, value):
        ref[:, z, :, columns] = value.astype(BF).reshape(12, 16, 256)

    for n in range(2):
        columns = pl.ds(n * 256, 256)
        act, slope_n = gelu_both(dot(k_ref[...], ef[:, columns]))
        act_b[:, columns] = act.astype(BF)
        slope[:, columns] = slope_n
        put(act_all, columns, rates * act)
    ring_a = Ring(w, p, lambda j: act_all.at[:, j])
    ring_a.start()
    spread1.relay()
    finish_weights()

    sum1 = Gather(w, p, parts, near, far, False)

    def wide(chip):
        return pl.ds(pl.multiple_of(chip * 256, 256), 256)

    sum1.compute(lambda chip: dot(act_b[...], rf[:, wide(chip)]))
    sum1.relay()
    ring_a.step(1)
    recon = sum1.finish()
    block_of(resid, m)[...] = (
        block_of(k_ref, m)[...].astype(F32) + recon - block_of(v_ref, m)[...].astype(F32)
    ).astype(BF)
    spread_r.start()
    ring_a.step(2)
    for n in range(2):
        columns = pl.ds(n * 256, 256)
        qe[:, columns] = dot(q_ref[...], ef[:, columns])
        cr[:, columns] = dot_nt(c_ref[...], rf[columns, :])
    spread_r.relay()
    spread1.finish()
    spread_r.finish()

    take_rows(r_rows, resid)
    ring_rows = Ring(w, p, lambda j: r_rows.at[j], cond=p.low)
    ring_rows.start()
    for n in range(2):
        columns = pl.ds(n * 256, 256)
        d_hidden = dot_nt(resid[...], rf[columns, :]) * slope[:, columns]
        put(dz_all, columns, rates * d_hidden)
    ring_z = Ring(w, p, lambda j: dz_all.at[:, j])
    ring_z.start()
    ring_a.step(3)
    for s in range(1, 5):
        ring_rows.step(s)
        if s == 4:
            score(c_ref, r_rows, score3)
            spread3.start()
            ring_a.step(4)
        ring_z.step(s)

    for n in range(2):
        columns = pl.ds(n * 256, 256)
        zq = qe[:, columns] - dot(score1[...], dz_all[:, :, :, columns].reshape(1536, 256))
        act, slope_n = gelu_both(zq)
        aq[:, columns] = act.astype(BF)
        slope[:, columns] = slope_n

    order = (4, -3, 3, -2, 2, -1, 1, 0)
    s_x = [w.slot() for _ in range(8)]
    for i, off in enumerate(order):
        block = mod(z + off, SEQ)
        both = dot_tn(aq[...], c_ref[:, wide(block)])
        g_r[0, block] = both[:, :128].astype(BF)
        g_r[1, block] = both[:, 128:].astype(BF)
        w.start(g_r.at[1 - d, block], x_r.at[block], s_x[i], p.partner)
    spread3.relay()

    sum2 = Gather(w, p, parts2, near2, far2, True)
    sum2.compute(
        lambda chip: dot_nt(aq[...], act_all[pl.ds(2 * chip, 2)].reshape(256, HID))
    )
    spread3.finish()

    for n in range(2):
        columns = pl.ds(n * 256, 256)
        d_act = cr[:, columns] - dot(score3[...], act_all[:, :, :, columns].reshape(1536, 256))
        dzq[:, columns] = (d_act * slope[:, columns]).astype(BF)
    fold_e = Fold(w, p, lambda j: g_e[j].astype(F32), up_e, down_e)
    fold_r = Fold(w, p, lambda j: x_r[j].astype(F32), up_r, down_r)
    for i, off in enumerate(order):
        block = mod(z + off, SEQ)
        g_e[block] = dot_tn(q_ref[:, wide(block)], dzq[...]).astype(BF)
        if i == 1:
            fold_e.start(g_e.at[mod(z + 4, SEQ)], g_e.at[mod(z - 3, SEQ)])

    def take(i):
        block = mod(z + order[i], SEQ)
        ref = x_r.at[block]
        w.arrive(ref, s_x[i], p.partner)
        ref[...] = (ref[...].astype(F32) + g_r[d, block].astype(F32)).astype(BF)

    take(0)
    take(1)
    fold_r.start(x_r.at[mod(z + 4, SEQ)], x_r.at[mod(z - 3, SEQ)])
    sum2.relay()
    fold_e.step(1)
    take(2)
    take(3)
    fold_r.step(1)

    def own_score():
        own2[...] = jnp.where(causal, sum2.finish(), 0.0).astype(BF)

    pl.when(p.low)(own_score)
    sum3 = Gather(w, p, parts3, near3, far3, False)

    def mixed_tile(chip):
        first = dot(aq[...], rf[:, wide(chip)])
        return first - dot(own2[...], r_rows[:, :, wide(chip)].reshape(128, 256))

    pl.when(jnp.logical_not(p.low))(lambda: clear(own2, r_rows))
    sum3.compute(mixed_tile)
    fold_e.step(2)
    take(4)
    take(5)
    fold_r.step(2)
    sum3.relay()
    fold_e.step(3)
    take(6)
    fold_r.step(3)
    total = fold_e.finish()
    x_e[0] = total[:128].astype(BF)
    x_e[1] = total[128:].astype(BF)
    s_swap = w.slot()
    w.start(x_e.at[1 - d], x_e.at[2], s_swap, p.partner)
    mixed_ref[...] = (block_of(q_ref, m)[...].astype(F32) + sum3.finish()).astype(BF)
    take(7)

    w.arrive(x_e.at[2], s_swap, p.partner)
    grad = x_e[d].astype(F32) + x_e[2].astype(F32)
    eu, em1, ev = adam_update(em_ref[...], e1_ref[...], e2_ref[...], grad)
    eu_ref[...], em1_ref[...], ev_ref[...] = eu, em1, ev
    w_e[...] = eu.astype(BF)
    ru, rm1, rv = adam_update(rm_ref[...], r1_ref[...], r2_ref[...], fold_r.finish())
    ru_ref[...], rm1_ref[...], rv_ref[...] = ru, rm1, rv
    w_r[...] = ru.astype(BF)
    keep_e = pltpu.make_async_copy(w_e, ew_ref.at[e_block(z, d), :], local.at[0])
    keep_r = pltpu.make_async_copy(w_r, rw_ref.at[:, e_block(z, d)], local.at[1])
    keep_e.start()
    keep_r.start()
    keep_e.wait()
    keep_r.wait()
    finish_weights = weights(ew_ref, rw_ref, w_e, w_r, lambda s: None)
    finish_weights()
    w.drain()


def clear(*refs):
    for ref in refs:
        ref[...] = jnp.zeros(ref.shape, ref.dtype)


def body(
    query_rows, key_rows, value_rows, cotangent, inner_rate,
    expand_master, reduce_master, expand_first, reduce_first, expand_second, reduce_second,
):
    vmem = pl.BlockSpec(memory_space=pltpu.VMEM)
    hbm = pl.BlockSpec(memory_space=pl.ANY)
    e_shape, r_shape = expand_master.shape, reduce_master.shape

    def bf(*shape):
        return pltpu.VMEM(shape, BF)

    def f32(*shape):
        return pltpu.VMEM(shape, F32)

    outs = pl.pallas_call(
        kernel,
        out_shape=[
            jax.ShapeDtypeStruct((ROWS, 128), BF),
            jax.ShapeDtypeStruct(e_shape, F32),
            jax.ShapeDtypeStruct(r_shape, F32),
            jax.ShapeDtypeStruct(e_shape, F32),
            jax.ShapeDtypeStruct(r_shape, F32),
            jax.ShapeDtypeStruct(e_shape, F32),
            jax.ShapeDtypeStruct(r_shape, F32),
            jax.ShapeDtypeStruct((D, HID), BF),
            jax.ShapeDtypeStruct((HID, D), BF),
        ],
        in_specs=[vmem] * 11,
        out_specs=[vmem] * 7 + [hbm] * 2,
        scratch_shapes=[
            bf(D, HID), bf(HID, D),
            bf(SEQ, 16, D), bf(SEQ, 16, D),
            bf(12, SEQ, 16, HID), bf(12, SEQ, 16, HID),
            bf(ROWS, 1536), bf(ROWS, 1536),
            bf(ROWS, HID), f32(ROWS, HID),
            bf(ROWS, D), f32(ROWS, HID), f32(ROWS, HID),
            bf(2, 8, ROWS, 128), bf(8, ROWS, 128), bf(8, ROWS, 128),
            bf(2, 6, ROWS, 128), bf(6, ROWS, 128), bf(8, ROWS, 128),
            bf(2, 8, ROWS, 128), bf(8, ROWS, 128), bf(8, ROWS, 128),
            bf(ROWS, 128), bf(ROWS, HID), bf(ROWS, HID),
            bf(2, SEQ, HID, 128), bf(SEQ, HID, 128), bf(4, HID, 128), bf(3, HID, 128),
            bf(SEQ, 256, HID), bf(3, 128, HID), bf(4, 256, HID), bf(3, 256, HID),
            bf(128, HID), bf(HID, 128),
            pltpu.SemaphoreType.DMA((N_SEMS,)),
            pltpu.SemaphoreType.DMA((N_SEMS,)),
            pltpu.SemaphoreType.DMA((2,)),
        ],
        compiler_params=pltpu.CompilerParams(
            collective_id=0, has_side_effects=True, vmem_limit_bytes=56 * 1024 * 1024
        ),
        cost_estimate=pl.CostEstimate(
            flops=5_000_000_000, bytes_accessed=12_000_000, transcendentals=400_000
        ),
    )(
        query_rows[0], key_rows[0], value_rows[0], cotangent[0], inner_rate,
        expand_master, reduce_master, expand_first, reduce_first, expand_second, reduce_second,
    )
    return (outs[0][None], *outs[1:])


def solution(mesh):
    in_specs = (
        P("dp", "seq", None),
        P("dp", "seq", None),
        P("dp", "seq", None),
        P("dp", "seq", None),
        P("dp", "seq"),
        P(("seq", "dp"), "mp"),
        P("mp", ("seq", "dp")),
        P(("seq", "dp"), "mp"),
        P("mp", ("seq", "dp")),
        P(("seq", "dp"), "mp"),
        P("mp", ("seq", "dp")),
    )
    out_specs = (
        P("dp", "seq", "mp"),
        P(("seq", "dp"), "mp"),
        P("mp", ("seq", "dp")),
        P(("seq", "dp"), "mp"),
        P("mp", ("seq", "dp")),
        P(("seq", "dp"), "mp"),
        P("mp", ("seq", "dp")),
        P(None, "mp"),
        P("mp", None),
    )
    return jax.shard_map(body, mesh=mesh, in_specs=in_specs, out_specs=out_specs, check_vma=False)
```

time: 1030 us -> 220 us (0.21)
  waiting for transfers between devices: 950 us -> 0 us
  Pallas kernels: 0 us -> 202 us
  matrix products: 43.7 us -> 0 us
  between operations: 14.4 us -> 0.68 us
  other arithmetic: 11.7 us -> 0 us
    all_gather x8 -> x0, waiting for transfers between devices: 535 us -> none  [the longest x1 84 us: body(): lax.all_gather(reduce_updated.astype(jnp.bfloat16), ('seq', 'dp'), axis=1...]
    reduce_scatter x3 -> x0, waiting for transfers between devices: 265 us -> none  [the longest x1 100 us: body(): lax.psum_scatter(expand_grad, ('seq', 'dp'), scatter_dimension=0, tiled=T...]
    pallas_call x0 -> x1, Pallas kernels: none -> 202 us  [body(): pl.pallas_call(kernel, out_shape=[jax.ShapeDtypeStruct((ROWS, 128), BF),...]
    psum x1 -> x0, waiting for transfers between devices: 148 us -> none  [body(): recon = lax.psum(partial_recon, 'mp')]
    dot_general x11 -> x0, matrix products: 43.7 us -> none  [the longest x1 6.35 us: body(): jnp.dot(second_score, all_resid, preferred_element_type=jnp.float32)]
  transfers between devices with their start and end apart: 12 -> 0, of which waited for: 12 -> 0; matrix products, arithmetic and copies ran while one was open for 5% -> 0% of each run, Pallas kernels for 0% -> 0%
where the time goes in v1:
time: 220 us; the launch traced here: 217 us
  Pallas kernels  202 us (92%)
  local copies, waits for them, and re-layouts  14.3 us (6%)
    pallas_call x1, Pallas kernels, body(): pl.pallas_call(kernel, out_shape=[jax.ShapeDtypeStruct((ROWS, 128), BF),...  202 us
    unnamed x15, local copies, waits for them, and re-layouts  14.3 us

profile of v1, /device:TPU:2, one launch (start us, length us, event | category | flops | bytes accessed | tf_op | source)
XLA Modules:
  0.0 217.3 jit_solution(7991336183795140588)
XLA Ops:
  0.6 202.3 %shard_map.178 = (bf16[192,128]{1,0:T(8,128)(2,1)}, f32[128,512]{1,0:T(8,128)}, f32[512,128]{1,0:T(8,128)}, f32[128,512]{1,0:T(8,128)}, f32[512,128]{1,0:T(8,128...) custom-call(bf16[192,2048]{1,0:T(8,128)(2,1)} %bitcast.6, ...), custom_call_target="tpu_custom_call" | custom-call | flops 5000000000 | bytes 12000000 | tf_op jit(solution)/shard_map/pallas_call | solution.py:547
  203.0 0.0 copy-start.2
  203.0 0.0 copy-start.1
  203.0 1.6 copy.29
  204.6 1.7 copy.30
  206.3 1.7 copy.31
  207.9 1.7 copy.32
  209.6 1.7 copy.33
  211.3 1.7 copy.34
  212.9 0.0 copy-done.2
  212.9 0.7 copy.35
  213.6 0.0 copy-done.1
  213.6 0.0 copy-start
  213.6 1.3 copy.36
  215.0 1.0 copy-done
  216.0 1.3 copy.37
Async XLA Ops:
  203.0 9.9 %copy-start.2 = (f32[512,128]{1,0:T(8,128)S(1)}, f32[512,128]{1,0:T(8,128)}, u32[]{:S(2)}) copy-start(f32[512,128]{1,0:T(8,128)} %get-tuple-element.42) | copy-start | bytes 786436
  203.0 10.6 %copy-start.1 = (bf16[2048,512]{1,0:T(8,128)(2,1)S(1)}, bf16[2048,512]{1,0:T(8,128)(2,1)}, u32[]{:S(2)}) copy-start(bf16[2048,512]{1,0:T(8,128)(2,1)} %get-tuple-element.43) | copy-start | bytes 6291460
  213.6 2.3 %copy-start = (bf16[512,2048]{1,0:T(8,128)(2,1)S(1)}, bf16[512,2048]{1,0:T(8,128)(2,1)}, u32[]{:S(2)}) copy-start(bf16[512,2048]{1,0:T(8,128)(2,1)} %get-tuple-element.44) | copy-start | bytes 6291460

commit v2 on v1

v2 whole, which is shorter than its diff:
```python
import jax
import jax.numpy as jnp
from jax import lax
from jax.experimental import pallas as pl
from jax.experimental.pallas import tpu as pltpu
from jax.sharding import PartitionSpec as P

STEP = 1000
MESH = pl.DeviceIdType.MESH
F32 = jnp.float32
BF = jnp.bfloat16

gelu_scale = 0.7978845608028654
gelu_cubic = 0.044715
beta_first = 0.9
beta_second = 0.999
learn_rate = 0.001
weight_decay = 0.1
adam_eps = 1e-08

SEQ, DP, MP = 8, 2, 16
ROWS, D, HID = 192, 2048, 512
N_SEMS = 288


def gelu_both(value):
    inner = jnp.tanh(gelu_scale * (value + gelu_cubic * value * value * value))
    act = 0.5 * value * (1.0 + inner)
    slope = 0.5 * (1.0 + inner) + 0.5 * value * (1.0 - inner * inner) * gelu_scale * (
        1.0 + 3.0 * gelu_cubic * value * value
    )
    return act, slope


def adam_update(master, first, second, grad):
    momentum = beta_first * first + (1.0 - beta_first) * grad
    variance = beta_second * second + (1.0 - beta_second) * grad * grad
    first_corr = 1.0 - beta_first**STEP
    second_corr = 1.0 - beta_second**STEP
    updated = master - learn_rate * (
        momentum / first_corr / (jnp.sqrt(variance / second_corr) + adam_eps)
        + weight_decay * master
    )
    return (updated, momentum, variance)


def dot(a, b):
    return jnp.dot(a, b, preferred_element_type=F32)


def dot_nt(a, b):
    return lax.dot_general(a, b, (((1,), (1,)), ((), ())), preferred_element_type=F32)


def dot_tn(a, b):
    return lax.dot_general(a, b, (((0,), (0,)), ((), ())), preferred_element_type=F32)


def mod(a, n):
    return lax.rem(a + 2 * n, n)


class Wire:
    def __init__(self, send, recv):
        self.send, self.recv, self.count, self.sent = send, recv, 0, []

    def slot(self, count=1):
        self.count += count
        assert self.count <= N_SEMS
        return self.count - count

    def copy(self, src, dst, slot, to):
        return pltpu.make_async_remote_copy(
            src_ref=src,
            dst_ref=dst,
            send_sem=self.send.at[slot],
            recv_sem=self.recv.at[slot],
            device_id=to,
            device_id_type=MESH,
        )

    def start(self, src, dst, slot, to, cond=None):
        def go():
            self.copy(src, dst, slot, to).start()

        guarded(cond, go)
        self.sent.append((src, dst, slot, to, cond))

    def arrive(self, dst, slot, to, cond=None):
        def go():
            self.copy(dst, dst, slot, to).wait_recv()

        guarded(cond, go)

    def drain(self):
        for src, dst, slot, to, cond in self.sent:
            guarded(cond, lambda: self.copy(src, dst, slot, to).wait_send())
        self.sent = []


def guarded(cond, go):
    if cond is None:
        go()
    else:
        pl.when(cond)(go)


class Place:
    def __init__(self):
        self.m = lax.axis_index("mp")
        self.z = lax.axis_index("seq")
        self.d = lax.axis_index("dp")
        self.core = lax.rem(self.m, 2)
        self.chip = self.m // 2
        self.sibling = {"mp": self.chip * 2 + 1 - self.core}
        self.partner = {"dp": 1 - self.d}
        self.up = {"seq": mod(self.z + 1, SEQ)}
        self.down = {"seq": mod(self.z - 1, SEQ)}
        self.low = self.chip < 6

    def peer(self, off):
        return lax.rem(self.chip + off, 8)

    def source(self, off):
        return lax.rem(self.chip + 8 - off, 8)

    def chip_id(self, chip):
        return {"mp": chip * 2 + self.core}


def span(base, half, size):
    if half is None:
        return pl.ds(base, size)
    return pl.ds(base + half * (size // 2), size // 2)


class Ring:
    def __init__(self, w, p, view, cond=None, on_block=None):
        self.w, self.p, self.view, self.cond, self.on_block = w, p, view, cond, on_block
        self.ups = [w.slot() for _ in range(4)]
        self.downs = [w.slot() for _ in range(4)]

    def start(self, src=None):
        ref = self.view(self.p.z, None)
        src = ref if src is None else src
        self.w.start(src, ref, self.ups[0], self.p.up, self.cond)
        self.w.start(src, ref, self.downs[0], self.p.down, self.cond)

    def hop(self, s, block, sems, to, half):
        now = half if s == 4 else None
        ref = self.view(block, now)
        self.w.arrive(ref, sems[s - 1], to, self.cond)
        if s < 4:
            later = self.view(block, half if s == 3 else None)
            self.w.start(later, later, sems[s], to, self.cond)
        if self.on_block:
            self.on_block(block, now, 2 * s - 1 + half)

    def step(self, s):
        z = self.p.z
        self.hop(s, mod(z - s, SEQ), self.ups, self.p.up, 0)
        self.hop(s, mod(z + s, SEQ), self.downs, self.p.down, 1)


class Share:
    def __init__(self, w, p, one_a, pair_a, one_b):
        self.w, self.p, self.one_a, self.one_b = w, p, one_a, one_b
        self.s_a = w.slot()
        self.s_b = [w.slot() for _ in range(9)]
        self.ring_a = Ring(w, p, pair_a)
        self.ring_b = Ring(
            w, p, lambda j, half: one_b(j, p.d, half), on_block=self.forward
        )

    def forward(self, block, half, index, src=None):
        ref = self.one_b(block, self.p.d, half)
        self.w.start(ref if src is None else src, ref, self.s_b[index], self.p.partner)

    def start_a(self, src):
        self.w.start(src, self.one_a(self.p.z, self.p.d), self.s_a, self.p.partner)

    def open_a(self):
        p = self.p
        self.w.arrive(self.one_a(p.z, 1 - p.d), self.s_a, p.partner)
        self.ring_a.start()

    def start_b(self, src):
        self.ring_b.start(src)
        self.forward(self.p.z, None, 0, src)

    def take_b(self, s):
        p = self.p
        if s == 0:
            self.w.arrive(self.one_b(p.z, 1 - p.d, None), self.s_b[0], p.partner)
            return
        for half, block in enumerate((mod(p.z - s, SEQ), mod(p.z + s, SEQ))):
            ref = self.one_b(block, 1 - p.d, half if s == 4 else None)
            self.w.arrive(ref, self.s_b[2 * s - 1 + half], p.partner)


class Spread:
    def __init__(self, w, p, view, low):
        self.w, self.p, self.view, self.low = w, p, view, low
        self.far = [w.slot() for _ in range(8)]
        self.near = [w.slot() for _ in range(8)]

    def cond(self, chip):
        return chip < 6 if self.low else None

    def start(self):
        w, p = self.w, self.p
        own = self.view(p.m)
        for off in range(1, 8):
            w.start(own, own, self.far[off], p.chip_id(p.peer(off)), self.cond(p.chip))
        w.start(own, own, self.near[0], p.sibling, self.cond(p.chip))

    def relay(self):
        w, p = self.w, self.p
        for off in range(1, 8):
            src = p.source(off)
            ref = self.view(src * 2 + p.core)
            w.arrive(ref, self.far[off], p.chip_id(p.peer(off)), self.cond(src))
            w.start(ref, ref, self.near[off], p.sibling, self.cond(src))

    def finish(self):
        w, p = self.w, self.p
        for off in range(8):
            src = p.source(off)
            ref = self.view(src * 2 + 1 - p.core)
            w.arrive(ref, self.near[off], p.sibling, self.cond(src))


class Gather:
    def __init__(self, w, p, parts, near, far, low):
        self.w, self.p, self.parts, self.near, self.far, self.low = w, p, parts, near, far, low
        self.s_near = w.slot(8)
        self.s_far = w.slot(8)

    def cond(self, chip):
        return chip < 6 if self.low else None

    def compute(self, chip, tile):
        def go():
            both = tile(chip)
            self.parts[0, chip] = both[:, :128].astype(BF)
            self.parts[1, chip] = both[:, 128:].astype(BF)

        guarded(self.cond(chip), go)
        self.w.start(
            self.parts.at[1 - self.p.core, chip],
            self.near.at[chip],
            self.s_near + chip,
            self.p.sibling,
            self.cond(chip),
        )

    def compute_all(self, tile):
        for off in (1, 2, 3, 4, 5, 6, 7, 0):
            self.compute(self.p.peer(off), tile)

    def relay(self):
        w, p = self.w, self.p
        for off in (1, 2, 3, 4, 5, 6, 7, 0):
            chip = p.peer(off)
            ref = self.near.at[chip]
            w.arrive(ref, self.s_near + chip, p.sibling, self.cond(chip))

            def go():
                total = ref[...].astype(F32) + self.parts[p.core, chip].astype(F32)
                self.near[chip] = total.astype(BF)

            guarded(self.cond(chip), go)
            if off:
                to = p.chip_id(chip)
                w.start(ref, self.far.at[off], self.s_far + off, to, self.cond(chip))

    def finish(self):
        w, p = self.w, self.p
        total = self.near[p.chip].astype(F32)
        for off in range(1, 8):
            w.arrive(self.far.at[off], self.s_far + off, p.chip_id(p.peer(off)))
            total = total + self.far[off].astype(F32)
        return total


class Fold:
    def __init__(self, w, p, own, up_half, down_half, ups, downs):
        self.w, self.p, self.own = w, p, own
        self.halves = (up_half, down_half)
        self.full = (ups, downs)
        self.sems = ([w.slot() for _ in range(4)], [w.slot() for _ in range(4)])

    def way(self, side):
        return self.p.down if side else self.p.up

    def start(self):
        for side in range(2):
            src = self.own(mod(self.p.z + 4, SEQ), side)
            self.w.start(src, self.halves[side], self.sems[side][0], self.way(side))

    def step(self, s):
        w = self.w
        for side in range(2):
            away = s - 4 if side else 4 - s
            block = mod(self.p.z + away, SEQ)
            out = self.full[side].at[s - 1]
            if s == 1:
                got, held = self.halves[side], self.own(block, side)
                w.arrive(got, self.sems[side][0], self.way(side))
                held[...] = (held[...].astype(F32) + got[...].astype(F32)).astype(BF)
                ref = self.own(block, None)
            else:
                ref, term = self.full[side].at[s - 2], self.own(block, None)
                w.arrive(ref, self.sems[side][s - 1], self.way(side))
                ref[...] = (ref[...].astype(F32) + term[...].astype(F32)).astype(BF)
            w.start(ref, out, self.sems[side][s], self.way(side))

    def finish(self):
        total = self.own(self.p.z, None)[...].astype(F32)
        for side in range(2):
            ref = self.full[side].at[2]
            self.w.arrive(ref, self.sems[side][3], self.way(side))
            total = total + ref[...].astype(F32)
        return total


def take_turns(*tasks):
    tasks = list(tasks)
    while tasks:
        for task in list(tasks):
            if next(task, "done") == "done":
                tasks.remove(task)


ORDER = (4, 3, -3, 2, -2, 1, -1, 0)


def kernel(
    q_in, k_in, v_in, c_in, rate_in,
    em_in, rm_in, e1_in, r1_in, e2_in, r2_in,
    mixed_ref, eu_ref, ru_ref, em1_ref, rm1_ref, ev_ref, rv_ref, ew_ref, rw_ref,
    q_ref, k_ref, v_ref, c_ref, rate_ref, em_ref, rm_ref, e1_ref, r1_ref, e2_ref, r2_ref,
    ef, rf, k_rows, r_rows, act_all, dz_all, score1, score3, act_b, slope, resid, qe, cr,
    parts, near, far, parts2, near2, far2, parts3, near3, far3, own2, aq, dzq,
    ga_e, gb_e, xb_e, ga_r, gb_r, xb_r, ha, hb_e, hb_r, fa, fb_e, fb_r, swap_e, swap_r,
    w_e, w_r, send, recv, local,
):
    w, p = Wire(send, recv), Place()
    m, z, d = p.m, p.z, p.d

    loads = {}
    for index, (src, dst) in enumerate(
        (
            (em_in, em_ref), (rm_in, rm_ref), (k_in, k_ref), (rate_in, rate_ref),
            (v_in, v_ref), (q_in, q_ref), (c_in, c_ref), (e1_in, e1_ref), (r1_in, r1_ref),
            (e2_in, e2_ref), (r2_in, r2_ref),
        )
    ):
        loads[index] = pltpu.make_async_copy(src, dst, local.at[index])
        loads[index].start()

    barrier = pltpu.get_barrier_semaphore()
    friends = [p.up, p.down, p.partner, p.sibling]
    friends += [p.chip_id(p.peer(off)) for off in range(1, 8)]
    for friend in friends:
        pl.semaphore_signal(barrier, inc=1, device_id=friend, device_id_type=MESH)
    pl.semaphore_wait(barrier, len(friends))

    def block_at(j, dd):
        return pl.multiple_of(j * 256 + dd * 128, 128)

    def pair_at(j):
        return pl.multiple_of(j * 256, 256)

    def share_e(full):
        return Share(
            w,
            p,
            lambda j, dd: full.at[pl.ds(block_at(j, dd), 128), 0:256],
            lambda j, half: full.at[span(pair_at(j), half, 256), 0:256],
            lambda j, dd, half: full.at[span(block_at(j, dd), half, 128), 256:512],
        )

    def share_r(full):
        return Share(
            w,
            p,
            lambda j, dd: full.at[0:256, pl.ds(block_at(j, dd), 128)],
            lambda j, half: full.at[span(0, half, 256), pl.ds(pair_at(j), 256)],
            lambda j, dd, half: full.at[span(256, half, 256), pl.ds(block_at(j, dd), 128)],
        )

    share1, share2 = share_e(ef), share_r(rf)
    loads[0].wait()
    ef[pl.ds(block_at(z, d), 128), :] = em_ref[...].astype(BF)
    share1.start_a(share1.one_a(z, d))
    share1.start_b(share1.one_b(z, d, None))
    loads[1].wait()
    rf[:, pl.ds(block_at(z, d), 128)] = rm_ref[...].astype(BF)
    share1.open_a()
    share2.start_a(share2.one_a(z, d))
    for index in (2, 3, 4, 5, 6):
        loads[index].wait()

    t_at = z * ROWS + lax.broadcasted_iota(jnp.int32, (ROWS, 128), 0)
    col = lax.broadcasted_iota(jnp.int32, (ROWS, 128), 1)
    s_at = (col // 16) * ROWS + m * 16 + lax.rem(col, 16)
    causal = t_at >= s_at
    eye = lax.broadcasted_iota(jnp.int32, (ROWS, ROWS), 0) == lax.broadcasted_iota(
        jnp.int32, (ROWS, ROWS), 1
    )
    rates = jnp.sum(jnp.where(eye, rate_ref[...], 0.0), axis=1, keepdims=True)

    own_rows = pl.ds(pl.multiple_of(m * 16, 16), 16)

    def take_rows(out, rows_ref):
        def go():
            out[z] = rows_ref[own_rows, :]

        guarded(p.low, go)

    def block_of(ref, block):
        return ref.at[:, pl.ds(pl.multiple_of(block * 128, 128), 128)]

    def wide(chip):
        return pl.ds(pl.multiple_of(chip * 256, 256), 256)

    spread1 = Spread(w, p, lambda b: block_of(score1, b), True)
    spread_r = Spread(w, p, lambda b: block_of(resid, b), False)
    spread3 = Spread(w, p, lambda b: block_of(score3, b), True)

    def score(rows_ref, others, out):
        def go():
            part = dot_nt(rows_ref[...], others[...].reshape(128, D))
            block_of(out, m)[...] = jnp.where(causal, part, 0.0).astype(BF)

        guarded(p.low, go)

    def put(ref, columns, value):
        ref[:, z, :, columns] = value.astype(BF).reshape(12, 16, 256)

    def rows_ring(ref):
        return Ring(w, p, lambda j, half: ref.at[j, :, span(0, half, D)], cond=p.low)

    def hidden_ring(ref):
        return Ring(w, p, lambda j, half: ref.at[span(0, half, 12), j])

    take_rows(k_rows, k_ref)
    ring_k, ring_rows = rows_ring(k_rows), rows_ring(r_rows)
    ring_a, ring_z = hidden_ring(act_all), hidden_ring(dz_all)

    def step1(s):
        share1.ring_a.step(s)
        share1.ring_b.step(s)

    def step2(s):
        share2.ring_a.step(s)
        share2.ring_b.step(s)

    step1(1)
    share2.start_b(share2.one_b(z, d, None))
    step1(2)
    share2.open_a()
    step1(3)
    step1(4)
    step2(1)
    for s in range(5):
        share1.take_b(s)

    for n in range(2):
        columns = pl.ds(n * 256, 256)
        act, slope_n = gelu_both(dot(k_ref[...], ef[:, columns]))
        act_b[:, columns] = act.astype(BF)
        slope[:, columns] = slope_n
        put(act_all, columns, rates * act)

    sum1 = Gather(w, p, parts, near, far, False)

    def recon_tile(chip):
        return dot(act_b[...], rf[:, wide(chip)])

    step2(2)
    share2.take_b(0)
    sum1.compute(z, recon_tile)
    step2(3)
    ring_a.start()
    ring_k.start()
    for s in (1, 2, 3):
        share2.take_b(s)
        sum1.compute(mod(z - s, SEQ), recon_tile)
        sum1.compute(mod(z + s, SEQ), recon_tile)
    step2(4)
    share2.take_b(4)
    sum1.compute(mod(z + 4, SEQ), recon_tile)
    sum1.relay()
    ring_a.step(1)
    ring_k.step(1)
    for n in range(2):
        columns = pl.ds(n * 256, 256)
        qe[:, columns] = dot(q_ref[...], ef[:, columns])
    recon = sum1.finish()
    block_of(resid, m)[...] = (
        block_of(k_ref, m)[...].astype(F32) + recon - block_of(v_ref, m)[...].astype(F32)
    ).astype(BF)
    spread_r.start()
    ring_a.step(2)
    ring_k.step(2)
    for n in range(2):
        columns = pl.ds(n * 256, 256)
        cr[:, columns] = dot_nt(c_ref[...], rf[columns, :])
    spread_r.relay()
    ring_a.step(3)
    ring_k.step(3)
    spread_r.finish()

    for n in range(2):
        columns = pl.ds(n * 256, 256)
        d_hidden = dot_nt(resid[...], rf[columns, :]) * slope[:, columns]
        put(dz_all, columns, rates * d_hidden)
    ring_z.start()
    take_rows(r_rows, resid)
    ring_rows.start()
    ring_a.step(4)
    ring_k.step(4)
    score(q_ref, k_rows, score1)
    spread1.start()
    ring_z.step(1)
    ring_rows.step(1)
    spread1.relay()
    ring_z.step(2)
    ring_rows.step(2)
    spread1.finish()
    ring_z.step(3)
    ring_rows.step(3)
    ring_z.step(4)

    for n in range(2):
        columns = pl.ds(n * 256, 256)
        zq = qe[:, columns] - dot(score1[...], dz_all[:, :, :, columns].reshape(1536, 256))
        act, slope_n = gelu_both(zq)
        aq[:, columns] = act.astype(BF)
        slope[:, columns] = slope_n

    s_xe, s_xr = [w.slot() for _ in range(8)], [w.slot() for _ in range(8)]
    fold_ar = Fold(
        w, p, lambda j, half: ga_r.at[j, span(0, half, 256)],
        ha.at[0], ha.at[1], fa.at[0], fa.at[1],
    )
    fold_ae = Fold(
        w, p, lambda j, half: ga_e.at[j, span(0, half, 256)],
        ha.at[2], ha.at[3], fa.at[2], fa.at[3],
    )
    fold_br = Fold(
        w, p, lambda j, half: xb_r.at[j, span(0, half, 256)],
        hb_r.at[0], hb_r.at[1], fb_r.at[0], fb_r.at[1],
    )
    fold_be = Fold(
        w, p, lambda j, half: xb_e.at[j, span(0, half, 128)],
        hb_e.at[0], hb_e.at[1], fb_e.at[0], fb_e.at[1],
    )
    for i, off in enumerate(ORDER):
        block = mod(z + off, SEQ)
        both = dot_tn(aq[...], c_ref[:, wide(block)])
        ga_r[block] = both[:256].astype(BF)
        gb_r[0, block] = both[256:, :128].astype(BF)
        gb_r[1, block] = both[256:, 128:].astype(BF)
        w.start(gb_r.at[1 - d, block], xb_r.at[block], s_xr[i], p.partner)
        if i == 0:
            fold_ar.start()
    ring_rows.step(4)
    score(c_ref, r_rows, score3)
    spread3.start()

    sum2 = Gather(w, p, parts2, near2, far2, True)
    sum2.compute_all(
        lambda chip: dot_nt(aq[...], act_all[pl.ds(2 * chip, 2)].reshape(256, HID))
    )
    spread3.relay()
    sum2.relay()
    fold_ar.step(1)
    spread3.finish()

    for n in range(2):
        columns = pl.ds(n * 256, 256)
        d_act = cr[:, columns] - dot(score3[...], act_all[:, :, :, columns].reshape(1536, 256))
        dzq[:, columns] = (d_act * slope[:, columns]).astype(BF)
    for i, off in enumerate(ORDER):
        block = mod(z + off, SEQ)
        both = dot_tn(q_ref[:, wide(block)], dzq[...])
        ga_e[block] = both[:, :256].astype(BF)
        gb_e[0, block] = both[:128, 256:].astype(BF)
        gb_e[1, block] = both[128:, 256:].astype(BF)
        w.start(gb_e.at[1 - d, block], xb_e.at[block], s_xe[i], p.partner)
        if i == 0:
            fold_ae.start()

    for index in (7, 8, 9, 10):
        loads[index].wait()
    share3, share4 = share_e(ew_ref), share_r(rw_ref)
    keeps = []

    def optimizer(is_e, part, grad):
        refs = (
            (em_ref, e1_ref, e2_ref, eu_ref, em1_ref, ev_ref, w_e)
            if is_e
            else (rm_ref, r1_ref, r2_ref, ru_ref, rm1_ref, rv_ref, w_r)
        )
        at = pl.ds(256 * part, 256)
        at = (slice(None), at) if is_e else (at, slice(None))
        outs = adam_update(refs[0][at], refs[1][at], refs[2][at], grad)
        refs[3][at], refs[4][at], refs[5][at] = outs
        refs[6][at] = outs[0].astype(BF)
        own = refs[6].at[at]
        share = share3 if is_e else share4
        home = share.one_b(z, d, None) if part else share.one_a(z, d)
        keep = pltpu.make_async_copy(own, home, local.at[11 + len(keeps)])
        keep.start()
        keeps.append(keep)
        return share, own, keep

    def part_a(is_e, fold, swap, first):
        for s in range(first, 4):
            fold.step(s)
            yield
        total = fold.finish()
        for dd in range(2):
            at = pl.ds(dd * 128, 128)
            swap[dd] = (total[128 * dd : 128 * dd + 128] if is_e else total[:, 128 * dd : 128 * dd + 128]).astype(BF)
        slot = w.slot()
        w.start(swap.at[1 - d], swap.at[2], slot, p.partner)
        yield
        w.arrive(swap.at[2], slot, p.partner)
        grad = swap[d].astype(F32) + swap[2].astype(F32)
        share, own, keep = optimizer(is_e, 0, grad)
        share.start_a(own)
        yield
        keep.wait()
        share.open_a()
        for s in range(1, 5):
            yield
            share.ring_a.step(s)

    def part_b(is_e, fold, mine, got, sems):
        def take(i):
            block = mod(z + ORDER[i], SEQ)
            ref = got.at[block]
            w.arrive(ref, sems[i], p.partner)
            ref[...] = (ref[...].astype(F32) + mine[d, block].astype(F32)).astype(BF)

        take(0)
        fold.start()
        yield
        for s in range(1, 4):
            take(2 * s - 1)
            take(2 * s)
            fold.step(s)
            yield
        take(7)
        share, own, keep = optimizer(is_e, 1, fold.finish())
        share.start_b(own)
        for s in range(1, 5):
            yield
            share.ring_b.step(s)
        for s in range(5):
            yield
            share.take_b(s)
        keep.wait()

    def output():
        pl.when(p.low)(own_score)
        pl.when(jnp.logical_not(p.low))(lambda: clear(own2, r_rows))
        sum3 = Gather(w, p, parts3, near3, far3, False)
        sum3.compute_all(mixed_tile)
        yield
        sum3.relay()
        yield
        mixed_ref[...] = (block_of(q_ref, m)[...].astype(F32) + sum3.finish()).astype(BF)

    def own_score():
        own2[...] = jnp.where(causal, sum2.finish(), 0.0).astype(BF)

    def mixed_tile(chip):
        first = dot(aq[...], rf[:, wide(chip)])
        return first - dot(own2[...], r_rows[:, :, wide(chip)].reshape(128, 256))

    take_turns(
        part_b(False, fold_br, gb_r, xb_r, s_xr),
        part_a(False, fold_ar, swap_r, 2),
        part_a(True, fold_ae, swap_e, 1),
        part_b(True, fold_be, gb_e, xb_e, s_xe),
        output(),
    )
    w.drain()


def clear(*refs):
    for ref in refs:
        ref[...] = jnp.zeros(ref.shape, ref.dtype)


def pass_on(*refs):
    *arrays, sems = refs
    count = len(arrays) // 3
    ins, outs = [], []
    for src, dst, held in zip(arrays[:count], arrays[count : 2 * count], arrays[2 * count :]):
        pieces = 4 if src.shape[0] * src.shape[1] > 100_000 else 1
        size = src.shape[0] // pieces
        for piece in range(pieces):
            rows = pl.ds(piece * size, size)
            index = len(ins)
            ins.append(pltpu.make_async_copy(src.at[rows], held.at[rows], sems.at[0, index]))
            outs.append(pltpu.make_async_copy(held.at[rows], dst.at[rows], sems.at[1, index]))
            ins[-1].start()
    for copy_in, copy_out in zip(ins, outs):
        copy_in.wait()
        copy_out.start()
    for copy_out in outs:
        copy_out.wait()


def body(
    query_rows, key_rows, value_rows, cotangent, inner_rate,
    expand_master, reduce_master, expand_first, reduce_first, expand_second, reduce_second,
):
    vmem = pl.BlockSpec(memory_space=pltpu.VMEM)
    hbm = pl.BlockSpec(memory_space=pl.ANY)
    e_shape, r_shape = expand_master.shape, reduce_master.shape

    def bf(*shape):
        return pltpu.VMEM(shape, BF)

    def f32(*shape):
        return pltpu.VMEM(shape, F32)

    outs = pl.pallas_call(
        kernel,
        out_shape=[
            jax.ShapeDtypeStruct((ROWS, 128), BF),
            jax.ShapeDtypeStruct(e_shape, F32),
            jax.ShapeDtypeStruct(r_shape, F32),
            jax.ShapeDtypeStruct(e_shape, F32),
            jax.ShapeDtypeStruct(r_shape, F32),
            jax.ShapeDtypeStruct(e_shape, F32),
            jax.ShapeDtypeStruct(r_shape, F32),
            jax.ShapeDtypeStruct((D, HID), BF),
            jax.ShapeDtypeStruct((HID, D), BF),
        ],
        in_specs=[hbm] * 11,
        out_specs=[vmem] * 7 + [hbm] * 2,
        scratch_shapes=[
            bf(ROWS, D), bf(ROWS, D), bf(ROWS, D), bf(ROWS, D), f32(1, ROWS),
            f32(*e_shape), f32(*r_shape), f32(*e_shape), f32(*r_shape), f32(*e_shape), f32(*r_shape),
            bf(D, HID), bf(HID, D),
            bf(SEQ, 16, D), bf(SEQ, 16, D),
            bf(12, SEQ, 16, HID), bf(12, SEQ, 16, HID),
            bf(ROWS, 1536), bf(ROWS, 1536),
            bf(ROWS, HID), f32(ROWS, HID),
            bf(ROWS, D), f32(ROWS, HID), f32(ROWS, HID),
            bf(2, 8, ROWS, 128), bf(8, ROWS, 128), bf(8, ROWS, 128),
            bf(2, 6, ROWS, 128), bf(6, ROWS, 128), bf(8, ROWS, 128),
            bf(2, 8, ROWS, 128), bf(8, ROWS, 128), bf(8, ROWS, 128),
            bf(ROWS, 128), bf(ROWS, HID), bf(ROWS, HID),
            bf(SEQ, 256, 256), bf(2, SEQ, 128, 256), bf(SEQ, 128, 256),
            bf(SEQ, 256, 256), bf(2, SEQ, 256, 128), bf(SEQ, 256, 128),
            bf(4, 128, 256), bf(2, 64, 256), bf(2, 128, 128),
            bf(4, 3, 256, 256), bf(2, 3, 128, 256), bf(2, 3, 256, 128),
            bf(3, 128, 256), bf(3, 256, 128),
            bf(128, HID), bf(HID, 128),
            pltpu.SemaphoreType.DMA((N_SEMS,)),
            pltpu.SemaphoreType.DMA((N_SEMS,)),
            pltpu.SemaphoreType.DMA((16,)),
        ],
        compiler_params=pltpu.CompilerParams(
            collective_id=0, has_side_effects=True, vmem_limit_bytes=56 * 1024 * 1024
        ),
        cost_estimate=pl.CostEstimate(
            flops=5_000_000_000, bytes_accessed=12_000_000, transcendentals=400_000
        ),
    )(
        query_rows[0], key_rows[0], value_rows[0], cotangent[0], inner_rate,
        expand_master, reduce_master, expand_first, reduce_first, expand_second, reduce_second,
    )
    outs = pl.pallas_call(
        pass_on,
        out_shape=[jax.ShapeDtypeStruct(out.shape, out.dtype) for out in outs],
        in_specs=[hbm] * 9,
        out_specs=[hbm] * 9,
        scratch_shapes=[pltpu.VMEM(out.shape, out.dtype) for out in outs]
        + [pltpu.SemaphoreType.DMA((2, 16))],
        compiler_params=pltpu.CompilerParams(vmem_limit_bytes=60 * 1024 * 1024),
        cost_estimate=pl.CostEstimate(flops=0, bytes_accessed=12_000_000, transcendentals=0),
    )(*outs)
    return (outs[0][None], *outs[1:])


def solution(mesh):
    in_specs = (
        P("dp", "seq", None),
        P("dp", "seq", None),
        P("dp", "seq", None),
        P("dp", "seq", None),
        P("dp", "seq"),
        P(("seq", "dp"), "mp"),
        P("mp", ("seq", "dp")),
        P(("seq", "dp"), "mp"),
        P("mp", ("seq", "dp")),
        P(("seq", "dp"), "mp"),
        P("mp", ("seq", "dp")),
    )
    out_specs = (
        P("dp", "seq", "mp"),
        P(("seq", "dp"), "mp"),
        P("mp", ("seq", "dp")),
        P(("seq", "dp"), "mp"),
        P("mp", ("seq", "dp")),
        P(("seq", "dp"), "mp"),
        P("mp", ("seq", "dp")),
        P(None, "mp"),
        P("mp", None),
    )
    return jax.shard_map(body, mesh=mesh, in_specs=in_specs, out_specs=out_specs, check_vma=False)
```

time: 220 us -> 191 us (0.87); the launches traced: 217 us -> 191 us
  local copies, waits for them, and re-layouts: 14.3 us -> 0 us
  Pallas kernels: 202 us -> 190 us
    pallas_call x1, Pallas kernels: 202 us -> 185 us  [body(): pl.pallas_call(kernel, out_shape=[jax.ShapeDtypeStruct((ROWS, 128), BF),...]
    unnamed x15 -> x0, local copies, waits for them, and re-layouts: 14.3 us -> none
    pallas_call x0 -> x1, Pallas kernels: none -> 5.26 us  [body(): pl.pallas_call(pass_on, out_shape=[jax.ShapeDtypeStruct(out.shape, out.dt...]
where the time goes in v2:
time: 191 us
  Pallas kernels  190 us (99%)
    pallas_call x1, Pallas kernels, body(): pl.pallas_call(kernel, out_shape=[jax.ShapeDtypeStruct((ROWS, 128), BF),...  185 us
    pallas_call x1, Pallas kernels, body(): pl.pallas_call(pass_on, out_shape=[jax.ShapeDtypeStruct(out.shape, out.dt...  5.26 us

profile of v2, /device:TPU:2, one launch (start us, length us, event | category | flops | bytes accessed | tf_op | source)
XLA Modules:
  0.0 190.6 jit_solution(7037062821065024190)
XLA Ops:
  0.6 184.5 %shard_map.178 = (bf16[192,128]{1,0:T(8,128)(2,1)}, f32[128,512]{1,0:T(8,128)}, f32[512,128]{1,0:T(8,128)}, f32[128,512]{1,0:T(8,128)}, f32[512,128]{1,0:T(8,128...) custom-call(bf16[192,2048]{1,0:T(8,128)(2,1)} %bitcast.5, ...), custom_call_target="tpu_custom_call" | custom-call | flops 5000000000 | bytes 12000000 | tf_op jit(solution)/shard_map/pallas_call | solution.py:735
  185.2 5.3 %shard_map.179 = (bf16[192,128]{1,0:T(8,128)(2,1)}, f32[128,512]{1,0:T(8,128)}, f32[512,128]{1,0:T(8,128)}, f32[128,512]{1,0:T(8,128)}, f32[512,128]{1,0:T(8,128...) custom-call(bf16[192,128]{1,0:T(8,128)(2,1)} %get-tuple-element.27.refs_0_, ...), custom_call_target="tpu_custom_call" | custom-call | bytes 12000000 | tf_op jit(solution)/shard_map/pallas_call | solution.py:783

commit v3 on v2

v3 whole, which is shorter than its diff:
```python
import jax
import jax.numpy as jnp
from jax import lax
from jax.experimental import pallas as pl
from jax.experimental.pallas import tpu as pltpu
from jax.sharding import PartitionSpec as P

STEP = 1000
MESH = pl.DeviceIdType.MESH
F32 = jnp.float32
BF = jnp.bfloat16

gelu_scale = 0.7978845608028654
gelu_cubic = 0.044715
beta_first = 0.9
beta_second = 0.999
learn_rate = 0.001
weight_decay = 0.1
adam_eps = 1e-08

SEQ, DP, MP = 8, 2, 16
ROWS, D, HID = 192, 2048, 512
N_RECV, N_SEND = 424, 64


def gelu_both(value):
    inner = jnp.tanh(gelu_scale * (value + gelu_cubic * value * value * value))
    act = 0.5 * value * (1.0 + inner)
    slope = 0.5 * (1.0 + inner) + 0.5 * value * (1.0 - inner * inner) * gelu_scale * (
        1.0 + 3.0 * gelu_cubic * value * value
    )
    return act, slope


def adam_update(master, first, second, grad):
    momentum = beta_first * first + (1.0 - beta_first) * grad
    variance = beta_second * second + (1.0 - beta_second) * grad * grad
    first_corr = 1.0 - beta_first**STEP
    second_corr = 1.0 - beta_second**STEP
    updated = master - learn_rate * (
        momentum / first_corr / (jnp.sqrt(variance / second_corr) + adam_eps)
        + weight_decay * master
    )
    return (updated, momentum, variance)


def dot(a, b):
    return jnp.dot(a, b, preferred_element_type=F32)


def dot_nt(a, b):
    return lax.dot_general(a, b, (((1,), (1,)), ((), ())), preferred_element_type=F32)


def dot_tn(a, b):
    return lax.dot_general(a, b, (((0,), (0,)), ((), ())), preferred_element_type=F32)


def mod(a, n):
    return lax.rem(a + 2 * n, n)


class Batch:
    def __init__(self, w, cond=None, counts=None):
        self.sem, self.rows, self.cond, self.counts = len(w.batches), 0, cond, counts
        w.batches.append(self)
        assert self.sem < N_SEND


class Wire:
    def __init__(self, send, recv, dummy):
        self.send, self.recv, self.dummy = send, recv, dummy
        self.count, self.batches = 0, []

    def slot(self, count=1):
        self.count += count
        assert self.count <= N_RECV
        return self.count - count

    def copy(self, src, dst, slot, to, out=0):
        return pltpu.make_async_remote_copy(
            src_ref=src,
            dst_ref=dst,
            send_sem=self.send.at[out],
            recv_sem=self.recv.at[slot],
            device_id=to,
            device_id_type=MESH,
        )

    def start(self, src, dst, slot, to, batch, cond=None):
        guarded(cond, lambda: self.copy(src, dst, slot, to, batch.sem).start())
        size = 1
        for extent in src.shape:
            size *= extent
        batch.rows += size // HID

    def arrive(self, dst, slot, to, cond=None):
        guarded(cond, lambda: self.copy(dst, dst, slot, to).wait_recv())

    def wait(self, sem, rows):
        ref = self.dummy.at[0:rows]
        pltpu.make_async_copy(ref, ref, sem).wait()

    def drain(self):
        for batch in self.batches:
            if not batch.rows:
                continue
            for cond, rows in batch.counts or ((batch.cond, batch.rows),):
                guarded(cond, lambda: self.wait(self.send.at[batch.sem], rows))


def guarded(cond, go):
    if cond is None:
        go()
    else:
        pl.when(cond)(go)


class Place:
    def __init__(self):
        self.m = lax.axis_index("mp")
        self.z = lax.axis_index("seq")
        self.d = lax.axis_index("dp")
        self.core = lax.rem(self.m, 2)
        self.chip = self.m // 2
        self.sibling = {"mp": self.chip * 2 + 1 - self.core}
        self.partner = {"dp": 1 - self.d}
        self.up = {"seq": mod(self.z + 1, SEQ)}
        self.down = {"seq": mod(self.z - 1, SEQ)}
        self.up2 = {"seq": mod(self.z + 2, SEQ)}
        self.down2 = {"seq": mod(self.z - 2, SEQ)}
        self.low = self.chip < 6

    def peer(self, off):
        return lax.rem(self.chip + off, 8)

    def source(self, off):
        return lax.rem(self.chip + 8 - off, 8)

    def others(self, rows):
        return ((self.low, 5 * rows), (jnp.logical_not(self.low), 6 * rows))

    def chip_id(self, chip):
        return {"mp": chip * 2 + self.core}


def span(base, part, size):
    if part is None:
        return pl.ds(base, size)
    i, n = part
    return pl.ds(base + i * (size // n), size // n)


class Ring:
    def __init__(self, w, p, view, chunks=1, cond=None, on_chunk=None):
        self.w, self.p, self.view, self.chunks = w, p, view, chunks
        self.cond, self.on_chunk, self.batch = cond, on_chunk, Batch(w, cond)
        self.sems = [[w.slot(4) for _ in range(chunks)] for _ in range(2)]
        self.to = (p.up, p.down)

    def part(self, c, half=None):
        return (c, self.chunks) if half is None else (2 * c + half, 2 * self.chunks)

    def start(self, src=None):
        for c in range(self.chunks):
            ref = self.view(self.p.z, self.part(c))
            for side in range(2):
                own = ref if src is None else src(self.part(c))
                self.w.start(own, ref, self.sems[side][c], self.to[side], self.batch, self.cond)

    def step(self, s):
        for c in range(self.chunks):
            for side in range(2):
                self.hop(s, c, side)

    def hop(self, s, c, side):
        block = mod(self.p.z + (s if side else -s), SEQ)
        now = self.part(c, side if s == 4 else None)
        ref, sem, to = self.view(block, now), self.sems[side][c], self.to[side]
        self.w.arrive(ref, sem + s - 1, to, self.cond)
        if s < 4:
            later = self.view(block, self.part(c, side if s == 3 else None))
            self.w.start(later, later, sem + s, to, self.batch, self.cond)
        if self.on_chunk:
            self.on_chunk(block, now)


class Leap:
    def __init__(self, w, p, view, cond):
        self.w, self.p, self.view, self.cond = w, p, view, cond
        self.batch = Batch(w, cond)
        self.sems = [w.slot(4) for _ in range(2)]
        self.to = ((p.up, p.up2), (p.down, p.down2))

    def start(self):
        ref = self.view(self.p.z, None)
        for far in (1, 0):
            for side in range(2):
                to = self.to[side][far]
                self.w.start(ref, ref, self.sems[side] + far, to, self.batch, self.cond)

    def take(self, side, index, away, half=None):
        block = mod(self.p.z + (away if side else -away), SEQ)
        ref = self.view(block, half)
        self.w.arrive(ref, self.sems[side] + index, self.to[side][0], self.cond)
        return block, ref

    def relay(self):
        for side in range(2):
            block, ref = self.take(side, 1, 2)
            one, two = self.to[side]
            self.w.start(ref, ref, self.sems[side] + 2, one, self.batch, self.cond)
            ref = self.view(block, (side, 2))
            self.w.start(ref, ref, self.sems[side] + 3, two, self.batch, self.cond)

    def finish(self):
        for side in range(2):
            self.take(side, 0, 1)
            self.take(side, 2, 3)
            self.take(side, 3, 4, (side, 2))


class Share:
    def __init__(self, w, p, one_a, one_b):
        self.w, self.p, self.one_a, self.one_b = w, p, one_a, one_b
        self.s_a, self.s_b, self.batch, self.batch_b = w.slot(), w.slot(), Batch(w), Batch(w)
        self.ring_a = Ring(w, p, lambda j, part: one_a(j, p.d, part), 2)
        self.ring_o = Ring(w, p, lambda j, part: one_a(j, 1 - p.d, part), 2)
        self.ring_b = Ring(
            w, p, lambda j, part: one_b(j, p.d, part), 2, on_chunk=self.forward
        )

    def forward(self, block, part):
        ref = self.one_b(block, self.p.d, part)
        self.w.start(ref, ref, self.s_b, self.p.partner, self.batch_b)

    def start(self, own_a, own_b):
        p = self.p
        self.w.start(own_a(None), self.one_a(p.z, p.d, None), self.s_a, p.partner, self.batch)
        self.ring_b.start(own_b)
        self.ring_a.start(own_a)

    def open(self, own_b):
        p = self.p
        self.w.start(own_b(None), self.one_b(p.z, p.d, None), self.s_b, p.partner, self.batch_b)
        self.w.arrive(self.one_a(p.z, 1 - p.d, None), self.s_a, p.partner)
        self.ring_o.start()

    def finish(self):
        self.w.wait(self.w.recv.at[self.s_b], self.batch_b.rows)


class Spread:
    def __init__(self, w, p, view, low):
        self.w, self.p, self.view, self.low = w, p, view, low
        self.far, self.near = w.slot(8), w.slot()
        self.out = Batch(w, self.cond(p.chip))
        self.relayed = Batch(w, counts=p.others(48) if low else None)

    def cond(self, chip):
        return chip < 6 if self.low else None

    def start(self):
        w, p = self.w, self.p
        own = self.view(p.m)
        for off in range(1, 8):
            to = p.chip_id(p.peer(off))
            w.start(own, own, self.far + off, to, self.out, self.cond(p.chip))
        w.start(own, own, self.near, p.sibling, self.out, self.cond(p.chip))

    def relay(self):
        w, p = self.w, self.p
        for off in range(1, 8):
            src = p.source(off)
            ref = self.view(src * 2 + p.core)
            w.arrive(ref, self.far + off, p.chip_id(p.peer(off)), self.cond(src))
            w.start(ref, ref, self.near, p.sibling, self.relayed, self.cond(src))

    def finish(self):
        self.w.wait(self.w.recv.at[self.near], 48 * (6 if self.low else 8))


class Gather:
    def __init__(self, w, p, parts, near, far, low):
        self.w, self.p, self.parts, self.near, self.far, self.low = w, p, parts, near, far, low
        self.s_near, self.s_far = w.slot(8), w.slot()
        self.out = Batch(w, counts=((None, 6 * 48),) if low else None)
        self.relayed = Batch(w, counts=p.others(48) if low else None)

    def cond(self, chip):
        return chip < 6 if self.low else None

    def compute(self, chip, tile):
        def go():
            both = tile(chip)
            self.parts[0, chip] = both[:, :128].astype(BF)
            self.parts[1, chip] = both[:, 128:].astype(BF)

        guarded(self.cond(chip), go)
        self.w.start(
            self.parts.at[1 - self.p.core, chip],
            self.near.at[chip],
            self.s_near + chip,
            self.p.sibling,
            self.out,
            self.cond(chip),
        )

    def compute_all(self, tile):
        for off in (1, 2, 3, 4, 5, 6, 7, 0):
            self.compute(self.p.peer(off), tile)

    def relay(self):
        w, p = self.w, self.p
        for off in (1, 2, 3, 4, 5, 6, 7, 0):
            chip = p.peer(off)
            ref = self.near.at[chip]
            w.arrive(ref, self.s_near + chip, p.sibling, self.cond(chip))

            def go():
                total = ref[...].astype(F32) + self.parts[p.core, chip].astype(F32)
                self.near[chip] = total.astype(BF)

            guarded(self.cond(chip), go)
            if off:
                to = p.chip_id(chip)
                w.start(ref, self.far.at[off], self.s_far, to, self.relayed, self.cond(chip))

    def finish(self):
        w, p = self.w, self.p
        total = self.near[p.chip].astype(F32)
        w.arrive(self.far.at[1:8], self.s_far, p.sibling)
        for off in range(1, 8):
            total = total + self.far[off].astype(F32)
        return total


class Fold:
    def __init__(self, w, p, own, halves, fulls, chunks):
        self.w, self.p, self.own, self.halves, self.fulls = w, p, own, halves, fulls
        self.chunks, self.batch = chunks, Batch(w)
        self.sems = [[w.slot(4) for _ in range(chunks)] for _ in range(2)]
        self.to = (p.up, p.down)

    def start(self):
        for c in range(self.chunks):
            for side in range(2):
                src = self.own(mod(self.p.z + 4, SEQ), (2 * c + side, 2 * self.chunks))
                dst = self.halves(side, (c, self.chunks))
                self.w.start(src, dst, self.sems[side][c], self.to[side], self.batch)

    def step(self, s):
        for c in range(self.chunks):
            for side in range(2):
                self.hop(s, c, side)

    def hop(self, s, c, side):
        part, sem, to = (c, self.chunks), self.sems[side][c], self.to[side]
        block = mod(self.p.z + (s - 4 if side else 4 - s), SEQ)
        if s == 1:
            got, held = self.halves(side, part), self.own(block, (2 * c + side, 2 * self.chunks))
            self.w.arrive(got, sem, to)
            held[...] = (held[...].astype(F32) + got[...].astype(F32)).astype(BF)
            ref = self.own(block, part)
        else:
            ref, term = self.fulls(side, s - 2, part), self.own(block, part)
            self.w.arrive(ref, sem + s - 1, to)
            ref[...] = (ref[...].astype(F32) + term[...].astype(F32)).astype(BF)
        self.w.start(ref, self.fulls(side, s - 1, part), sem + s, to, self.batch)

    def finish(self):
        total = self.own(self.p.z, None)[...].astype(F32)
        for side in range(2):
            for c in range(self.chunks):
                ref = self.fulls(side, 2, (c, self.chunks))
                self.w.arrive(ref, self.sems[side][c] + 3, self.to[side])
            total = total + self.fulls(side, 2, None)[...].astype(F32)
        return total


class Twin:
    def __init__(self, w, p, ref):
        self.w, self.p, self.ref = w, p, ref
        self.slots, self.batch = (w.slot(), w.slot()), Batch(w)

    def rows(self, base, core):
        return self.ref.at[pl.ds(pl.multiple_of(base + core * 96, 32), 96)]

    def start(self):
        p = self.p
        to = self.rows(ROWS, p.core)
        self.w.start(self.rows(0, p.core), to, self.slots[0], p.partner, self.batch)

    def relay(self):
        p, ref = self.p, self.rows(ROWS, self.p.core)
        self.w.arrive(ref, self.slots[0], p.partner)
        self.w.start(ref, ref, self.slots[1], p.sibling, self.batch)

    def finish(self):
        self.w.arrive(self.rows(ROWS, 1 - self.p.core), self.slots[1], self.p.sibling)


def take_turns(*tasks):
    tasks = list(tasks)
    while tasks:
        for task in list(tasks):
            if next(task, "done") == "done":
                tasks.remove(task)


ORDER = (4, 3, -3, 2, -2, 1, -1, 0)


def kernel(
    q_in, k_in, v_in, c_in, rate_in,
    em_in, rm_in, e1_in, r1_in, e2_in, r2_in,
    mixed_ref, eu_ref, ru_ref, em1_ref, rm1_ref, ev_ref, rv_ref, ew_ref, rw_ref,
    q_ref, k_ref, v_ref, c_ref, rate_ref, em_ref, rm_ref, e1_ref, r1_ref, e2_ref, r2_ref,
    ef, rf, k_rows, r_rows, act_all, dz_all, score1, score3, act_b, slope, resid, qe, cr,
    parts, near, far, parts2, near2, far2, parts3, near3, far3, score2, aq, dzq,
    aq2, dzq2, g_e, g_r, half_buf, full_buf, swap_e, swap_r,
    w_e, w_r, send, recv, local,
):
    w, p = Wire(send, recv, ef), Place()
    m, z, d = p.m, p.z, p.d
    swaps = Batch(w)

    loads = {}
    for index, (src, dst) in enumerate(
        (
            (em_in, em_ref), (rm_in, rm_ref), (k_in, k_ref), (rate_in, rate_ref),
            (v_in, v_ref), (q_in, q_ref.at[0:ROWS]), (c_in, c_ref.at[0:ROWS]), (e1_in, e1_ref), (r1_in, r1_ref),
            (e2_in, e2_ref), (r2_in, r2_ref),
        )
    ):
        loads[index] = pltpu.make_async_copy(src, dst, local.at[index])
        loads[index].start()

    barrier = pltpu.get_barrier_semaphore()
    friends = [p.up, p.down, p.up2, p.down2, p.partner, p.sibling]
    friends += [p.chip_id(p.peer(off)) for off in range(1, 8)]
    for friend in friends:
        pl.semaphore_signal(barrier, inc=1, device_id=friend, device_id_type=MESH)
    pl.semaphore_wait(barrier, len(friends))

    def block_at(j, dd):
        return pl.multiple_of(j * 256 + dd * 128, 128)

    def share_e(full):
        def block(j, dd, part, columns):
            return full.at[span(block_at(j, dd), part, 128), columns]

        return Share(
            w,
            p,
            lambda j, dd, part: block(j, dd, part, slice(0, 256)),
            lambda j, dd, part: block(j, dd, part, slice(256, 512)),
        )

    def share_r(full):
        def block(j, dd, part, base):
            return full.at[span(base, part, 256), pl.ds(block_at(j, dd), 128)]

        return Share(
            w,
            p,
            lambda j, dd, part: block(j, dd, part, 0),
            lambda j, dd, part: block(j, dd, part, 256),
        )

    own_rows = pl.ds(pl.multiple_of(m * 16, 16), 16)

    def take_rows(out, rows_ref):
        def go():
            out[z] = rows_ref[own_rows, :]

        guarded(p.low, go)

    def rows_view(ref):
        return lambda j, part: ref.at[j, :, span(0, part, D)]

    share1, share2 = share_e(ef), share_r(rf)
    ring_k = Ring(w, p, rows_view(k_rows), cond=p.low)
    loads[0].wait()
    ef[pl.ds(block_at(z, d), 128), :] = em_ref[...].astype(BF)
    own1 = [lambda part: share1.one_a(z, d, part), lambda part: share1.one_b(z, d, part)]
    own2 = [lambda part: share2.one_a(z, d, part), lambda part: share2.one_b(z, d, part)]
    share1.start(*own1)
    loads[1].wait()
    rf[:, pl.ds(block_at(z, d), 128)] = rm_ref[...].astype(BF)
    share2.start(*own2)
    loads[2].wait()
    take_rows(k_rows, k_ref)
    ring_k.start()
    share1.open(own1[1])
    share2.open(own2[1])
    t_at = z * ROWS + lax.broadcasted_iota(jnp.int32, (ROWS, 128), 0)
    col = lax.broadcasted_iota(jnp.int32, (ROWS, 128), 1)
    s_at = (col // 16) * ROWS + m * 16 + lax.rem(col, 16)
    causal = t_at >= s_at
    eye = lax.broadcasted_iota(jnp.int32, (ROWS, ROWS), 0) == lax.broadcasted_iota(
        jnp.int32, (ROWS, ROWS), 1
    )
    loads[3].wait()
    rates = jnp.sum(jnp.where(eye, rate_ref[...], 0.0), axis=1, keepdims=True)


    def block_of(ref, block):
        return ref.at[:, pl.ds(pl.multiple_of(block * 128, 128), 128)]

    def wide(chip):
        return pl.ds(pl.multiple_of(chip * 256, 256), 256)

    spread1 = Spread(w, p, lambda b: block_of(score1, b), True)
    spread_r = Spread(w, p, lambda b: block_of(resid, b), False)
    spread3 = Spread(w, p, lambda b: block_of(score3, b), True)

    def score(rows_ref, others, out):
        def go():
            part = dot_nt(rows_ref[0:ROWS], others[...].reshape(128, D))
            block_of(out, m)[...] = jnp.where(causal, part, 0.0).astype(BF)

        guarded(p.low, go)

    def put(ref, columns, value):
        ref[:, z, :, columns] = value.astype(BF).reshape(12, 16, 256)

    def hidden_ring(ref, chunks):
        return Ring(w, p, lambda j, part: ref.at[span(0, part, 12), j], chunks)

    leap = Leap(w, p, rows_view(r_rows), p.low)
    ring_a, ring_z = hidden_ring(act_all, 3), hidden_ring(dz_all, 6)

    for s in range(1, 5):
        ring_k.step(s)
        for share in (share1, share2):
            share.ring_b.step(s)
        for share in (share1, share2):
            share.ring_a.step(s)
        for share in (share1, share2):
            share.ring_o.step(s)
    for index in (4, 5, 6):
        loads[index].wait()
    share1.finish()

    for n in range(2):
        columns = pl.ds(n * 256, 256)
        act, slope_n = gelu_both(dot(k_ref[...], ef[:, columns]))
        act_b[:, columns] = act.astype(BF)
        slope[:, columns] = slope_n
        put(act_all, columns, rates * act)

    ring_a.start()
    share2.finish()

    sum1 = Gather(w, p, parts, near, far, False)
    sum1.compute_all(lambda chip: dot(act_b[...], rf[:, wide(chip)]))
    sum1.relay()
    for n in range(2):
        columns = pl.ds(n * 256, 256)
        qe[:, columns] = dot(q_ref[0:ROWS], ef[:, columns])
    ring_a.step(1)
    recon = sum1.finish()
    block_of(resid, m)[...] = (
        block_of(k_ref, m)[...].astype(F32) + recon - block_of(v_ref, m)[...].astype(F32)
    ).astype(BF)
    spread_r.start()
    for n in range(2):
        columns = pl.ds(n * 256, 256)
        cr[:, columns] = dot_nt(c_ref[0:ROWS], rf[columns, :])
    ring_a.step(2)
    score(q_ref, k_rows, score1)
    spread_r.relay()
    ring_a.step(3)
    spread_r.finish()

    take_rows(r_rows, resid)
    for n in range(2):
        columns = pl.ds(n * 256, 256)
        d_hidden = dot_nt(resid[...], rf[columns, :]) * slope[:, columns]
        put(dz_all, columns, rates * d_hidden)
    ring_z.start()
    spread1.start()
    twin_q, twin_c = Twin(w, p, q_ref), Twin(w, p, c_ref)
    twin_c.start()
    ring_a.step(4)
    ring_z.step(1)
    spread1.relay()
    twin_q.start()
    ring_z.step(2)
    ring_z.step(3)
    leap.start()
    spread1.finish()
    twin_c.relay()
    ring_z.step(4)

    for n in range(2):
        columns = pl.ds(n * 256, 256)
        zq = qe[:, columns] - dot(score1[...], dz_all[:, :, :, columns].reshape(1536, 256))
        act, slope_n = gelu_both(zq)
        aq[:, columns] = act.astype(BF)
        slope[:, columns] = slope_n

    theirs = pl.ds(pl.multiple_of((1 - d) * 256, 256), 256)
    mine = pl.ds(pl.multiple_of(d * 256, 256), 256)
    s_aq, s_dzq = w.slot(), w.slot()
    w.start(aq.at[:, theirs], aq2.at[1], s_aq, p.partner, swaps)
    aq2[0] = aq[:, mine]
    sum2 = Gather(w, p, parts2, near2, far2, True)
    sum2.compute_all(
        lambda chip: dot_nt(aq[...], act_all[pl.ds(2 * chip, 2)].reshape(256, HID))
    )

    def fold_of(ref, k):
        return Fold(
            w,
            p,
            lambda j, part: ref.at[j, span(0, part, 256)],
            lambda side, part: half_buf.at[2 * k + side, span(0, part, 128)],
            lambda side, s, part: full_buf.at[2 * k + side, s, span(0, part, 256)],
            4,
        )

    fold_r, fold_e = fold_of(g_r, 0), fold_of(g_e, 1)
    leap.relay()
    twin_c.finish()
    w.arrive(aq2.at[1], s_aq, p.partner)
    for i, off in enumerate(ORDER):
        block = mod(z + off, SEQ)
        g_r[block] = dot_tn(aq2[...].reshape(2 * ROWS, 256), c_ref[:, wide(block)]).astype(BF)
        if i == 0:
            fold_r.start()
    leap.finish()
    score(c_ref, r_rows, score3)
    spread3.start()
    twin_q.relay()
    fold_r.step(1)
    spread3.relay()
    fold_r.step(2)
    spread3.finish()
    for n in range(2):
        columns = pl.ds(n * 256, 256)
        d_act = cr[:, columns] - dot(score3[...], act_all[:, :, :, columns].reshape(1536, 256))
        dzq[:, columns] = (d_act * slope[:, columns]).astype(BF)
    w.start(dzq.at[:, theirs], dzq2.at[1], s_dzq, p.partner, swaps)
    dzq2[0] = dzq[:, mine]
    sum2.relay()
    fold_r.step(3)
    twin_q.finish()
    w.arrive(dzq2.at[1], s_dzq, p.partner)
    for i, off in enumerate(ORDER):
        block = mod(z + off, SEQ)
        g_e[block] = dot_tn(q_ref[:, wide(block)], dzq2[...].reshape(2 * ROWS, 256)).astype(BF)
        if i == 0:
            fold_e.start()

    for index in (7, 8, 9, 10):
        loads[index].wait()
    share3, share4 = share_e(ew_ref), share_r(rw_ref)
    def optimizer(is_e, half, grad):
        refs = (
            (em_ref, e1_ref, e2_ref, eu_ref, em1_ref, ev_ref, w_e)
            if is_e
            else (rm_ref, r1_ref, r2_ref, ru_ref, rm1_ref, rv_ref, w_r)
        )
        at = pl.ds(pl.multiple_of(256 * half, 256), 256)
        at = (slice(None), at) if is_e else (at, slice(None))
        outs = adam_update(refs[0][at], refs[1][at], refs[2][at], grad)
        refs[3][at], refs[4][at], refs[5][at] = outs
        refs[6][at] = outs[0].astype(BF)

    def matrix(is_e, fold, swap, first):
        for s in range(first, 4):
            fold.step(s)
            yield
        total = fold.finish()
        for dd in range(2):
            at = slice(128 * dd, 128 * dd + 128)
            swap[dd] = (total[at] if is_e else total[:, at]).astype(BF)
        slot = w.slot()
        w.start(swap.at[1 - d], swap.at[2], slot, p.partner, swaps)
        optimizer(is_e, d, swap[d].astype(F32))
        yield
        w.arrive(swap.at[2], slot, p.partner)
        optimizer(is_e, 1 - d, swap[2].astype(F32))
        share = share3 if is_e else share4
        own = w_e if is_e else w_r

        def own_a(part):
            return own.at[span(0, part, 128), 0:256] if is_e else own.at[span(0, part, 256)]

        def own_b(part):
            return own.at[span(0, part, 128), 256:512] if is_e else own.at[span(256, part, 256)]

        share.start(own_a, own_b)
        keeps = []
        for src, dst in ((own_a, share.one_a), (own_b, share.one_b)):
            index = 11 + len(keeps) + 2 * is_e
            keeps.append(pltpu.make_async_copy(src(None), dst(z, d, None), local.at[index]))
            keeps[-1].start()
        yield
        share.open(own_b)
        for s in range(1, 5):
            yield
            share.ring_b.step(s)
            share.ring_a.step(s)
            share.ring_o.step(s)
        for keep in keeps:
            keep.wait()
        yield
        share.finish()

    def output():
        pl.when(p.low)(own_score)
        pl.when(jnp.logical_not(p.low))(lambda: clear(score2, r_rows))
        sum3 = Gather(w, p, parts3, near3, far3, False)
        sum3.compute_all(mixed_tile)
        yield
        sum3.relay()
        yield
        mixed_ref[...] = (block_of(q_ref, m)[0:ROWS].astype(F32) + sum3.finish()).astype(BF)

    def own_score():
        score2[...] = jnp.where(causal, sum2.finish(), 0.0).astype(BF)

    def mixed_tile(chip):
        first = dot(aq[...], rf[:, wide(chip)])
        return first - dot(score2[...], r_rows[:, :, wide(chip)].reshape(128, 256))

    take_turns(
        matrix(False, fold_r, swap_r, 4),
        matrix(True, fold_e, swap_e, 1),
        output(),
    )
    w.drain()


def clear(*refs):
    for ref in refs:
        ref[...] = jnp.zeros(ref.shape, ref.dtype)


def pass_on(*refs):
    *arrays, sems = refs
    count = len(arrays) // 3
    ins, outs = [], []
    for src, dst, held in zip(arrays[:count], arrays[count : 2 * count], arrays[2 * count :]):
        pieces = 4 if src.shape[0] * src.shape[1] > 100_000 else 1
        size = src.shape[0] // pieces
        for piece in range(pieces):
            rows = pl.ds(piece * size, size)
            index = len(ins)
            ins.append(pltpu.make_async_copy(src.at[rows], held.at[rows], sems.at[0, index]))
            outs.append(pltpu.make_async_copy(held.at[rows], dst.at[rows], sems.at[1, index]))
            ins[-1].start()
    for copy_in, copy_out in zip(ins, outs):
        copy_in.wait()
        copy_out.start()
    for copy_out in outs:
        copy_out.wait()


def body(
    query_rows, key_rows, value_rows, cotangent, inner_rate,
    expand_master, reduce_master, expand_first, reduce_first, expand_second, reduce_second,
):
    vmem = pl.BlockSpec(memory_space=pltpu.VMEM)
    hbm = pl.BlockSpec(memory_space=pl.ANY)
    e_shape, r_shape = expand_master.shape, reduce_master.shape

    def bf(*shape):
        return pltpu.VMEM(shape, BF)

    def f32(*shape):
        return pltpu.VMEM(shape, F32)

    outs = pl.pallas_call(
        kernel,
        out_shape=[
            jax.ShapeDtypeStruct((ROWS, 128), BF),
            jax.ShapeDtypeStruct(e_shape, F32),
            jax.ShapeDtypeStruct(r_shape, F32),
            jax.ShapeDtypeStruct(e_shape, F32),
            jax.ShapeDtypeStruct(r_shape, F32),
            jax.ShapeDtypeStruct(e_shape, F32),
            jax.ShapeDtypeStruct(r_shape, F32),
            jax.ShapeDtypeStruct((D, HID), BF),
            jax.ShapeDtypeStruct((HID, D), BF),
        ],
        in_specs=[hbm] * 11,
        out_specs=[vmem] * 7 + [hbm] * 2,
        scratch_shapes=[
            bf(2 * ROWS, D), bf(ROWS, D), bf(ROWS, D), bf(2 * ROWS, D), f32(1, ROWS),
            f32(*e_shape), f32(*r_shape), f32(*e_shape), f32(*r_shape), f32(*e_shape), f32(*r_shape),
            bf(D, HID), bf(HID, D),
            bf(SEQ, 16, D), bf(SEQ, 16, D),
            bf(12, SEQ, 16, HID), bf(12, SEQ, 16, HID),
            bf(ROWS, 1536), bf(ROWS, 1536),
            bf(ROWS, HID), f32(ROWS, HID),
            bf(ROWS, D), f32(ROWS, HID), f32(ROWS, HID),
            bf(2, 8, ROWS, 128), bf(8, ROWS, 128), bf(8, ROWS, 128),
            bf(2, 6, ROWS, 128), bf(6, ROWS, 128), bf(8, ROWS, 128),
            bf(2, 8, ROWS, 128), bf(8, ROWS, 128), bf(8, ROWS, 128),
            bf(ROWS, 128), bf(ROWS, HID), bf(ROWS, HID),
            bf(2, ROWS, 256), bf(2, ROWS, 256),
            bf(SEQ, 256, 256), bf(SEQ, 256, 256),
            bf(4, 128, 256), bf(4, 3, 256, 256),
            bf(3, 128, 256), bf(3, 256, 128),
            bf(128, HID), bf(HID, 128),
            pltpu.SemaphoreType.DMA((N_SEND,)),
            pltpu.SemaphoreType.DMA((N_RECV,)),
            pltpu.SemaphoreType.DMA((16,)),
        ],
        compiler_params=pltpu.CompilerParams(
            collective_id=0, has_side_effects=True, vmem_limit_bytes=56 * 1024 * 1024
        ),
        cost_estimate=pl.CostEstimate(
            flops=5_000_000_000, bytes_accessed=12_000_000, transcendentals=400_000
        ),
    )(
        query_rows[0], key_rows[0], value_rows[0], cotangent[0], inner_rate,
        expand_master, reduce_master, expand_first, reduce_first, expand_second, reduce_second,
    )
    outs = pl.pallas_call(
        pass_on,
        out_shape=[jax.ShapeDtypeStruct(out.shape, out.dtype) for out in outs],
        in_specs=[hbm] * 9,
        out_specs=[hbm] * 9,
        scratch_shapes=[pltpu.VMEM(out.shape, out.dtype) for out in outs]
        + [pltpu.SemaphoreType.DMA((2, 16))],
        compiler_params=pltpu.CompilerParams(vmem_limit_bytes=60 * 1024 * 1024),
        cost_estimate=pl.CostEstimate(flops=0, bytes_accessed=12_000_000, transcendentals=0),
    )(*outs)
    return (outs[0][None], *outs[1:])


def solution(mesh):
    in_specs = (
        P("dp", "seq", None),
        P("dp", "seq", None),
        P("dp", "seq", None),
        P("dp", "seq", None),
        P("dp", "seq"),
        P(("seq", "dp"), "mp"),
        P("mp", ("seq", "dp")),
        P(("seq", "dp"), "mp"),
        P("mp", ("seq", "dp")),
        P(("seq", "dp"), "mp"),
        P("mp", ("seq", "dp")),
    )
    out_specs = (
        P("dp", "seq", "mp"),
        P(("seq", "dp"), "mp"),
        P("mp", ("seq", "dp")),
        P(("seq", "dp"), "mp"),
        P("mp", ("seq", "dp")),
        P(("seq", "dp"), "mp"),
        P("mp", ("seq", "dp")),
        P(None, "mp"),
        P("mp", None),
    )
    return jax.shard_map(body, mesh=mesh, in_specs=in_specs, out_specs=out_specs, check_vma=False)
```

time: 191 us -> 165 us (0.86)
  Pallas kernels: 190 us -> 165 us
    pallas_call x1, Pallas kernels: 185 us -> 159 us  [body(): pl.pallas_call(kernel, out_shape=[jax.ShapeDtypeStruct((ROWS, 128), BF),...]
where the time goes in v3:
time: 165 us
  Pallas kernels  165 us (100%)
    pallas_call x1, Pallas kernels, body(): pl.pallas_call(kernel, out_shape=[jax.ShapeDtypeStruct((ROWS, 128), BF),...  159 us
    pallas_call x1, Pallas kernels, body(): pl.pallas_call(pass_on, out_shape=[jax.ShapeDtypeStruct(out.shape, out.dt...  5.26 us

profile of v3, /device:TPU:2, one launch (start us, length us, event | category | flops | bytes accessed | tf_op | source)
XLA Modules:
  0.0 165.3 jit_solution(7714905648599197046)
XLA Ops:
  0.6 159.3 %shard_map.178 = (bf16[192,128]{1,0:T(8,128)(2,1)}, f32[128,512]{1,0:T(8,128)}, f32[512,128]{1,0:T(8,128)}, f32[128,512]{1,0:T(8,128)}, f32[512,128]{1,0:T(8,128...) custom-call(bf16[192,2048]{1,0:T(8,128)(2,1)} %bitcast.5, ...), custom_call_target="tpu_custom_call" | custom-call | flops 5000000000 | bytes 12000000 | tf_op jit(solution)/shard_map/pallas_call | solution.py:777
  159.9 5.3 %shard_map.179 = (bf16[192,128]{1,0:T(8,128)(2,1)}, f32[128,512]{1,0:T(8,128)}, f32[512,128]{1,0:T(8,128)}, f32[128,512]{1,0:T(8,128)}, f32[512,128]{1,0:T(8,128...) custom-call(bf16[192,128]{1,0:T(8,128)(2,1)} %get-tuple-element.27.refs_0_, ...), custom_call_target="tpu_custom_call" | custom-call | bytes 12000000 | tf_op jit(solution)/shard_map/pallas_call | solution.py:824

commit v4 on v3

--- a/solution.py
+++ b/solution.py
@@ -20,7 +20,7 @@
 
 SEQ, DP, MP = 8, 2, 16
 ROWS, D, HID = 192, 2048, 512
-N_RECV, N_SEND = 424, 64
+N_RECV, N_SEND = 314, 41
 
 
 def gelu_both(value):
@@ -152,10 +152,10 @@
 
 
 class Ring:
-    def __init__(self, w, p, view, chunks=1, cond=None, on_chunk=None):
+    def __init__(self, w, p, view, chunks=1, cond=None, on_chunk=None, like=None):
         self.w, self.p, self.view, self.chunks = w, p, view, chunks
         self.cond, self.on_chunk, self.batch = cond, on_chunk, Batch(w, cond)
-        self.sems = [[w.slot(4) for _ in range(chunks)] for _ in range(2)]
+        self.sems = like.sems if like else [[w.slot(4) for _ in range(chunks)] for _ in range(2)]
         self.to = (p.up, p.down)
 
     def part(self, c, half=None):
@@ -221,13 +221,15 @@
 
 
 class Share:
-    def __init__(self, w, p, one_a, one_b):
+    def __init__(self, w, p, one_a, one_b, like=None):
         self.w, self.p, self.one_a, self.one_b = w, p, one_a, one_b
-        self.s_a, self.s_b, self.batch, self.batch_b = w.slot(), w.slot(), Batch(w), Batch(w)
-        self.ring_a = Ring(w, p, lambda j, part: one_a(j, p.d, part), 2)
-        self.ring_o = Ring(w, p, lambda j, part: one_a(j, 1 - p.d, part), 2)
+        self.s_a, self.s_b = (like.s_a, like.s_b) if like else (w.slot(), w.slot())
+        self.batch, self.batch_b = Batch(w), Batch(w)
+        earlier = (like.ring_a, like.ring_o, like.ring_b) if like else (None, None, None)
+        self.ring_a = Ring(w, p, lambda j, part: one_a(j, p.d, part), 2, like=earlier[0])
+        self.ring_o = Ring(w, p, lambda j, part: one_a(j, 1 - p.d, part), 2, like=earlier[1])
         self.ring_b = Ring(
-            w, p, lambda j, part: one_b(j, p.d, part), 2, on_chunk=self.forward
+            w, p, lambda j, part: one_b(j, p.d, part), 2, on_chunk=self.forward, like=earlier[2]
         )
 
     def forward(self, block, part):
@@ -446,7 +448,7 @@
     def block_at(j, dd):
         return pl.multiple_of(j * 256 + dd * 128, 128)
 
-    def share_e(full):
+    def share_e(full, like=None):
         def block(j, dd, part, columns):
             return full.at[span(block_at(j, dd), part, 128), columns]
 
@@ -455,17 +457,19 @@
             p,
             lambda j, dd, part: block(j, dd, part, slice(0, 256)),
             lambda j, dd, part: block(j, dd, part, slice(256, 512)),
+            like,
         )
 
-    def share_r(full):
-        def block(j, dd, part, base):
-            return full.at[span(base, part, 256), pl.ds(block_at(j, dd), 128)]
+    def share_r(full, like=None):
+        def block(j, dd, part, base, size):
+            return full.at[span(base, part, size), pl.ds(block_at(j, dd), 128)]
 
         return Share(
             w,
             p,
-            lambda j, dd, part: block(j, dd, part, 0),
-            lambda j, dd, part: block(j, dd, part, 256),
+            lambda j, dd, part: block(j, dd, part, 0, 192),
+            lambda j, dd, part: block(j, dd, part, 192, 320),
+            like,
         )
 
     own_rows = pl.ds(pl.multiple_of(m * 16, 16), 16)
@@ -489,9 +493,6 @@
     loads[1].wait()
     rf[:, pl.ds(block_at(z, d), 128)] = rm_ref[...].astype(BF)
     share2.start(*own2)
-    loads[2].wait()
-    take_rows(k_rows, k_ref)
-    ring_k.start()
     share1.open(own1[1])
     share2.open(own2[1])
     t_at = z * ROWS + lax.broadcasted_iota(jnp.int32, (ROWS, 128), 0)
@@ -532,14 +533,13 @@
     ring_a, ring_z = hidden_ring(act_all, 3), hidden_ring(dz_all, 6)
 
     for s in range(1, 5):
-        ring_k.step(s)
         for share in (share1, share2):
             share.ring_b.step(s)
         for share in (share1, share2):
             share.ring_a.step(s)
         for share in (share1, share2):
             share.ring_o.step(s)
-    for index in (4, 5, 6):
+    for index in (2, 4, 5, 6):
         loads[index].wait()
     share1.finish()
 
@@ -551,6 +551,8 @@
         put(act_all, columns, rates * act)
 
     ring_a.start()
+    take_rows(k_rows, k_ref)
+    ring_k.start()
     share2.finish()
 
     sum1 = Gather(w, p, parts, near, far, False)
@@ -560,6 +562,7 @@
         columns = pl.ds(n * 256, 256)
         qe[:, columns] = dot(q_ref[0:ROWS], ef[:, columns])
     ring_a.step(1)
+    ring_k.step(1)
     recon = sum1.finish()
     block_of(resid, m)[...] = (
         block_of(k_ref, m)[...].astype(F32) + recon - block_of(v_ref, m)[...].astype(F32)
@@ -569,9 +572,10 @@
         columns = pl.ds(n * 256, 256)
         cr[:, columns] = dot_nt(c_ref[0:ROWS], rf[columns, :])
     ring_a.step(2)
-    score(q_ref, k_rows, score1)
+    ring_k.step(2)
     spread_r.relay()
     ring_a.step(3)
+    ring_k.step(3)
     spread_r.finish()
 
     take_rows(r_rows, resid)
@@ -580,32 +584,34 @@
         d_hidden = dot_nt(resid[...], rf[columns, :]) * slope[:, columns]
         put(dz_all, columns, rates * d_hidden)
     ring_z.start()
-    spread1.start()
     twin_q, twin_c = Twin(w, p, q_ref), Twin(w, p, c_ref)
     twin_c.start()
     ring_a.step(4)
+    ring_k.step(4)
+    score(q_ref, k_rows, score1)
+    spread1.start()
     ring_z.step(1)
-    spread1.relay()
     twin_q.start()
     ring_z.step(2)
+    spread1.relay()
     ring_z.step(3)
     leap.start()
     spread1.finish()
     twin_c.relay()
     ring_z.step(4)
 
-    for n in range(2):
-        columns = pl.ds(n * 256, 256)
+    theirs = pl.ds(pl.multiple_of((1 - d) * 256, 256), 256)
+    mine = pl.ds(pl.multiple_of(d * 256, 256), 256)
+    s_aq, s_dzq = w.slot(), w.slot()
+    for columns in (theirs, mine):
         zq = qe[:, columns] - dot(score1[...], dz_all[:, :, :, columns].reshape(1536, 256))
         act, slope_n = gelu_both(zq)
         aq[:, columns] = act.astype(BF)
         slope[:, columns] = slope_n
-
-    theirs = pl.ds(pl.multiple_of((1 - d) * 256, 256), 256)
-    mine = pl.ds(pl.multiple_of(d * 256, 256), 256)
-    s_aq, s_dzq = w.slot(), w.slot()
-    w.start(aq.at[:, theirs], aq2.at[1], s_aq, p.partner, swaps)
+        if columns is theirs:
+            w.start(aq.at[:, theirs], aq2.at[1], s_aq, p.partner, swaps)
     aq2[0] = aq[:, mine]
+
     sum2 = Gather(w, p, parts2, near2, far2, True)
     sum2.compute_all(
         lambda chip: dot_nt(aq[...], act_all[pl.ds(2 * chip, 2)].reshape(256, HID))
@@ -638,11 +644,11 @@
     spread3.relay()
     fold_r.step(2)
     spread3.finish()
-    for n in range(2):
-        columns = pl.ds(n * 256, 256)
+    for columns in (theirs, mine):
         d_act = cr[:, columns] - dot(score3[...], act_all[:, :, :, columns].reshape(1536, 256))
         dzq[:, columns] = (d_act * slope[:, columns]).astype(BF)
-    w.start(dzq.at[:, theirs], dzq2.at[1], s_dzq, p.partner, swaps)
+        if columns is theirs:
+            w.start(dzq.at[:, theirs], dzq2.at[1], s_dzq, p.partner, swaps)
     dzq2[0] = dzq[:, mine]
     sum2.relay()
     fold_r.step(3)
@@ -656,7 +662,7 @@
 
     for index in (7, 8, 9, 10):
         loads[index].wait()
-    share3, share4 = share_e(ew_ref), share_r(rw_ref)
+    share3, share4 = share_e(ew_ref, share1), share_r(rw_ref, share2)
     def optimizer(is_e, half, grad):
         refs = (
             (em_ref, e1_ref, e2_ref, eu_ref, em1_ref, ev_ref, w_e)
@@ -687,10 +693,10 @@
         own = w_e if is_e else w_r
 
         def own_a(part):
-            return own.at[span(0, part, 128), 0:256] if is_e else own.at[span(0, part, 256)]
+            return own.at[span(0, part, 128), 0:256] if is_e else own.at[span(0, part, 192)]
 
         def own_b(part):
-            return own.at[span(0, part, 128), 256:512] if is_e else own.at[span(256, part, 256)]
+            return own.at[span(0, part, 128), 256:512] if is_e else own.at[span(192, part, 320)]
 
         share.start(own_a, own_b)
         keeps = []
@@ -745,7 +751,7 @@
     count = len(arrays) // 3
     ins, outs = [], []
     for src, dst, held in zip(arrays[:count], arrays[count : 2 * count], arrays[2 * count :]):
-        pieces = 4 if src.shape[0] * src.shape[1] > 100_000 else 1
+        pieces = 8 if src.shape[0] * src.shape[1] > 100_000 else 1
         size = src.shape[0] // pieces
         for piece in range(pieces):
             rows = pl.ds(piece * size, size)
@@ -827,7 +833,7 @@
         in_specs=[hbm] * 9,
         out_specs=[hbm] * 9,
         scratch_shapes=[pltpu.VMEM(out.shape, out.dtype) for out in outs]
-        + [pltpu.SemaphoreType.DMA((2, 16))],
+        + [pltpu.SemaphoreType.DMA((2, 23))],
         compiler_params=pltpu.CompilerParams(vmem_limit_bytes=60 * 1024 * 1024),
         cost_estimate=pl.CostEstimate(flops=0, bytes_accessed=12_000_000, transcendentals=0),
     )(*outs)

time: 165 us -> 160 us (0.970)
  Pallas kernels: 165 us -> 159 us
    pallas_call x1, Pallas kernels: 159 us -> 153 us  [body(): pl.pallas_call(kernel, out_shape=[jax.ShapeDtypeStruct((ROWS, 128), BF),...]
where the time goes in v4:
time: 160 us; the launch traced here: 159 us
  Pallas kernels  159 us (99%)
    pallas_call x1, Pallas kernels, body(): pl.pallas_call(kernel, out_shape=[jax.ShapeDtypeStruct((ROWS, 128), BF),...  153 us
    pallas_call x1, Pallas kernels, body(): pl.pallas_call(pass_on, out_shape=[jax.ShapeDtypeStruct(out.shape, out.dt...  5.36 us

profile of v4, /device:TPU:2, one launch (start us, length us, event | category | flops | bytes accessed | tf_op | source)
XLA Modules:
  0.0 159.5 jit_solution(16658208821982746885)
XLA Ops:
  0.6 153.3 %shard_map.178 = (bf16[192,128]{1,0:T(8,128)(2,1)}, f32[128,512]{1,0:T(8,128)}, f32[512,128]{1,0:T(8,128)}, f32[128,512]{1,0:T(8,128)}, f32[512,128]{1,0:T(8,128...) custom-call(bf16[192,2048]{1,0:T(8,128)(2,1)} %bitcast.5, ...), custom_call_target="tpu_custom_call" | custom-call | flops 5000000000 | bytes 12000000 | tf_op jit(solution)/shard_map/pallas_call | solution.py:783
  153.9 5.4 %shard_map.179 = (bf16[192,128]{1,0:T(8,128)(2,1)}, f32[128,512]{1,0:T(8,128)}, f32[512,128]{1,0:T(8,128)}, f32[128,512]{1,0:T(8,128)}, f32[512,128]{1,0:T(8,128...) custom-call(bf16[192,128]{1,0:T(8,128)(2,1)} %get-tuple-element.27.refs_0_, ...), custom_call_target="tpu_custom_call" | custom-call | bytes 12000000 | tf_op jit(solution)/shard_map/pallas_call | solution.py:830
